TPU v7x, 256 devices: a whole 4x4x8 slice. The times are simulated.
256 devices in a mesh: img: 8 (over z_hi, x), txt: 32 (over z_lo, y, core).
Axes of the slice: x: 4, y: 4, z: 8 (z_hi: 2, z_lo: 4; z = z_hi * 4 + z_lo), core: 2. Of those that a mesh axis runs over, the one named last changes fastest.
Arguments:
- image_emb: bfloat16 [20480, 1152], P(('img', 'txt'))
- text_emb: bfloat16 [20480, 1152], P(('txt', 'img'))
- partner: int32 [20480], P('img'), may hold values from 0 to 20479, as said below
- log_scale: float32 [1], replicated, may hold values from 2 to 3
- bias: float32 [1], replicated, may hold values from -6 to -2
Outputs:
- loss: float32 [1], replicated
- grad_image: float32 [20480, 1152], P(('img', 'txt'))
- grad_text: float32 [20480, 1152], P(('txt', 'img'))
Inputs may be any that keep to these rules, and one draw needn't show every extreme that they name: partner is a permutation: each text row is paired with exactly one image row.
All inputs are finite; a program needn't handle non-finite values.
Results may differ from a plain program's by a relative error of at most 0.00099.
Values may be sent and summed in bfloat16 or wider, within the bound.
A program may use at most 64 MiB of HBM per device.

v0:
```python
import jax
import jax.numpy as jnp
from jax import lax
from jax.sharding import PartitionSpec as P


def normalize(emb):
    full = emb.astype(jnp.float32)
    inverse = lax.rsqrt(jnp.sum(full * full, axis=1, keepdims=True) + 1e-06)
    return (full * inverse, inverse)


def back_norm(unit, inverse, direction):
    inner = jnp.sum(unit * direction, axis=1, keepdims=True)
    return inverse * (direction - unit * inner)


def on_device(image_emb, text_emb, partner, log_scale, bias):
    rows = image_emb.shape[0]
    image_unit, image_inv = normalize(image_emb)
    text_unit, text_inv = normalize(text_emb)
    image_wire = image_unit.astype(jnp.bfloat16)
    text_wire = text_unit.astype(jnp.bfloat16)
    scale = jnp.exp(log_scale[0])
    shift = bias[0]
    texts = lax.all_gather(text_wire, "img", axis=0, tiled=True)
    text_count = texts.shape[0]
    columns = lax.axis_index("txt") * text_count + lax.iota(jnp.int32, text_count)
    piece = lax.all_gather(image_wire, "txt", axis=0, tiled=True)
    cosine = jnp.einsum("pd,qd->pq", piece, texts, preferred_element_type=jnp.float32)
    logits = scale * cosine + shift
    positive = (partner[:, None] == columns[None, :]).astype(jnp.float32)
    signed = 2.0 * positive - 1.0
    part_loss = jnp.sum(jax.nn.softplus(-signed * logits))
    slope = (jax.nn.sigmoid(logits) - positive).astype(jnp.bfloat16)
    text_part = jnp.einsum("pq,pd->qd", slope, piece, preferred_element_type=jnp.float32)
    part_loss, slope, text_part = (part_loss, slope, text_part)
    image_part = jnp.dot(slope, texts, preferred_element_type=jnp.float32)
    image_sum = lax.psum_scatter(image_part, "txt", scatter_dimension=0, tiled=True)
    text_sum = lax.psum_scatter(text_part, "img", scatter_dimension=0, tiled=True)
    loss_total = lax.psum(part_loss, ("img", "txt"))
    total_pairs = rows * lax.axis_size("img") * lax.axis_size("txt")
    loss = (loss_total / total_pairs).reshape(1)
    grad_image = back_norm(image_unit, image_inv, scale * image_sum)
    grad_text = back_norm(text_unit, text_inv, scale * text_sum)
    return (loss, grad_image, grad_text)


def solution(mesh):
    return jax.shard_map(
        on_device,
        mesh=mesh,
        in_specs=(P(("img", "txt"), None), P(("txt", "img"), None), P("img"), P(), P()),
        out_specs=(P(), P(("img", "txt"), None), P(("txt", "img"), None)),
        check_vma=False,
    )
```

profile of v0, /device:TPU:1, one launch (start us, length us, event | category | flops | bytes accessed | tf_op | source)
XLA Modules:
  0.0 442.8 jit_solution(10205453797075738348)
XLA Ops:
  7.2 0.0 all-gather.5.cloned.1.call-start
  7.2 1.1 fusion.19
  8.3 1.7 fusion.8
  10.0 0.0 all-gather.5.cloned.1.call-update
  10.0 0.0 all-gather.3.cloned.1.call-start
  10.1 1.1 fusion.15
  11.1 1.7 fusion.11
  12.8 0.0 all-gather.3.cloned.1.call-update
  12.9 0.0 reduce-scatter.5.cloned.1.call-start
  14.3 67.1 %all-gather.5.cloned.1.call-done = bf16[640,1152]{1,0:T(8,128)(2,1)} async-done(((bf16[80,1152]{1,0:T(8,128)(2,1)}), bf16[640,1152]{1,0:T(8,128)(2,1)}) %all-gather.5.cloned.1.call-update) | async-done | bytes 1474576 | tf_op jit(solution)/shard_map/all_gather | solution.py:26
  81.3 65.9 %all-gather.3.cloned.1.call-done = bf16[2560,1152]{1,0:T(8,128)(2,1)} async-done(((bf16[80,1152]{1,0:T(8,128)(2,1)}), bf16[2560,1152]{1,0:T(8,128)(2,1)}) %all-gather.3.cloned.1.call-update) | async-done | bytes 5898256 | tf_op jit(solution)/shard_map/all_gather | solution.py:29
  147.3 13.1 %fusion.4 = (bf16[2560,640]{1,0:T(8,128)(2,1)S(1)}, f32[]{:T(128)}) fusion(f32[]{:T(128)} %bitcast.9, f32[]{:T(128)} %bitcast, s32[640]{0:T(1024)S(1)} %iota_add_fusion, s32[2560]{0:T(1024)} %param.7, bf16[2560,1152]{1,0:T(8,128)(2,1)} %all-gather.3.cloned.1.call-done, bf16[640,1152]{1,0:T(8,128)(2,1)} %all-gather.5.cloned.1.call-done), kind=kOutput, calls=%fused_computation.7 | convolution fusion | flops 3807641600 | bytes 10662412 | tf_op jit(solution)/shard_map/pd,qd->pq/dot_general | solution.py:30
  160.4 1.8 copy-done.4
  162.2 6.2 %fusion.21 = f32[640,1152]{1,0:T(8,128)} fusion(bf16[2560,640]{1,0:T(8,128)(2,1)S(1)} %get-tuple-element.3, bf16[2560,1152]{1,0:T(8,128)(2,1)S(1)} %copy-done.2), kind=kOutput, calls=%fused_computation.32 | convolution fusion | flops 3774873600 | bytes 12124160 | tf_op jit(solution)/shard_map/pq,pd->qd/dot_general | solution.py:36
  168.3 0.0 reduce-scatter.5.cloned.1.call-update
  168.4 0.2 reduce-scatter.3.cloned.1.call-start
  168.6 9.3 %fusion.20 = f32[2560,1152]{1,0:T(8,128)} fusion(bf16[2560,640]{1,0:T(8,128)(2,1)} %copy-done.4, bf16[640,1152]{1,0:T(8,128)(2,1)S(1)} %copy-done.3), kind=kOutput, calls=%fused_computation.31 | convolution fusion | flops 3774873600 | bytes 16547840 | tf_op jit(solution)/shard_map/dot_general | solution.py:38
  177.9 84.3 %psum.7 = f32[]{:T(128)} all-reduce(f32[]{:T(128)} %get-tuple-element.4), channel_id=1, replica_groups=mesh['img'=8,'txt'=32] {'img','txt'}, use_global_device_ids=true, to_apply=%region_3.4 | all-reduce | flops 1 | bytes 8 | tf_op jit(solution)/shard_map/psum | solution.py:41
  262.9 11.4 %reduce-scatter.5.cloned.1.call-done = f32[80,1152]{1,0:T(8,128)} async-done(((f32[640,1152]{1,0:T(8,128)}), f32[80,1152]{1,0:T(8,128)}) %reduce-scatter.5.cloned.1.call-update) | async-done | bytes 368656 | tf_op jit(solution)/shard_map/reduce_scatter | solution.py:40
  274.3 1.2 fusion.16
  275.5 1.9 fusion.18
  277.4 154.7 %reduce-scatter.3.cloned.1.call-done = f32[80,1152]{1,0:T(8,128)} async-done(((f32[2560,1152]{1,0:T(8,128)}), f32[80,1152]{1,0:T(8,128)}) %reduce-scatter.3.cloned.1.call-update) | async-done | bytes 368656 | tf_op jit(solution)/shard_map/reduce_scatter | solution.py:39
  432.0 1.2 fusion.12
  433.3 1.9 fusion.14
  (13 shorter events, 0.0 us)
Async XLA Ops:
  7.2 74.2 %all-gather.5.cloned.1.call-start = ((), (), s32[]{:S(2)}) async-start(), calls=%async_computation.3 | async-start | bytes 1658880 | tf_op jit(solution)/shard_map/all_gather | solution.py:26
  10.0 137.2 %all-gather.3.cloned.1.call-start = ((), (), s32[]{:S(2)}) async-start(), calls=%async_computation.2 | async-start | bytes 6082560 | tf_op jit(solution)/shard_map/all_gather | solution.py:29
  12.9 261.4 %reduce-scatter.5.cloned.1.call-start = ((), (), s32[]{:S(2)}) async-start(), calls=%async_computation.5 | async-start | bytes 3317760 | tf_op jit(solution)/shard_map/reduce_scatter | solution.py:40
  147.3 14.9 %copy-start.2 = (bf16[2560,1152]{1,0:T(8,128)(2,1)S(1)}, bf16[2560,1152]{1,0:T(8,128)(2,1)}, u32[]{:S(2)}) copy-start(bf16[2560,1152]{1,0:T(8,128)(2,1)} %all-gather.3.cloned.1.call-done) | copy-start | bytes 17694724
  160.4 1.8 copy-start.4
  162.2 6.4 %copy-start.3 = (bf16[640,1152]{1,0:T(8,128)(2,1)S(1)}, bf16[640,1152]{1,0:T(8,128)(2,1)}, u32[]{:S(2)}) copy-start(bf16[640,1152]{1,0:T(8,128)(2,1)} %all-gather.5.cloned.1.call-done) | copy-start | bytes 4423684
  168.4 263.7 %reduce-scatter.3.cloned.1.call-start = ((), (), s32[]{:S(2)}) async-start(), calls=%async_computation.4 | async-start | bytes 12165120 | tf_op jit(solution)/shard_map/reduce_scatter | solution.py:39
  177.9 96.4 %copy-start = (bf16[80,1152]{1,0:T(8,128)(2,1)S(1)}, bf16[80,1152]{1,0:T(8,128)(2,1)}, u32[]{:S(2)}) copy-start(bf16[80,1152]{1,0:T(8,128)(2,1)} %param.6) | copy-start | bytes 552964
  177.9 254.1 %copy-start.1 = (bf16[80,1152]{1,0:T(8,128)(2,1)S(1)}, bf16[80,1152]{1,0:T(8,128)(2,1)}, u32[]{:S(2)}) copy-start(bf16[80,1152]{1,0:T(8,128)(2,1)} %param.5) | copy-start | bytes 552964
Sparse Core Ops, SparseCore 0:
  11.2 70.1 all-gather.4
  83.8 63.4 all-gather.2
  168.5 105.7 reduce-scatter.4
  276.7 155.2 reduce-scatter.2
where the time goes:
time: 448 us; the launch traced here: 443 us
  waiting for transfers between devices  299 us (67%)
  blocking collectives  84.3 us (19%)
  matrix products  28.6 us (6%)
  between operations  16.9 us (4%)
  other arithmetic  11.7 us (3%)
    reduce_scatter x1, waiting for transfers between devices, on_device(): lax.psum_scatter(image_part, 'txt', scatter_dimension=0, tiled=True)  155 us
    psum x1, blocking collectives, on_device(): loss_total = lax.psum(part_loss, ('img', 'txt'))  84.3 us
    all_gather x1, waiting for transfers between devices, on_device(): texts = lax.all_gather(text_wire, 'img', axis=0, tiled=True)  67.1 us
    all_gather x1, waiting for transfers between devices, on_device(): piece = lax.all_gather(image_wire, 'txt', axis=0, tiled=True)  65.9 us
    dot_general x1, matrix products, on_device(): jnp.einsum('pd,qd->pq', piece, texts, preferred_element_type=jnp.float32)  13.1 us
    reduce_scatter x1, waiting for transfers between devices, on_device(): lax.psum_scatter(text_part, 'img', scatter_dimension=0, tiled=True)  11.4 us
    dot_general x1, matrix products, on_device(): image_part = jnp.dot(slope, texts, preferred_element_type=jnp.float32)  9.32 us
  transfers between devices with their start and end apart: 4, of which 4 were waited for; matrix products, arithmetic and copies ran while one was open for 3% of the time, Pallas kernels for 0%

commit v1 on v0

v1 whole, which is shorter than its diff:
```python
import functools
import math

import jax
import jax.numpy as jnp
from jax import lax
from jax.experimental import pallas as pl
from jax.experimental.pallas import tpu as pltpu
from jax.sharding import PartitionSpec as P

MESH = pl.DeviceIdType.MESH
F32, BF16 = jnp.float32, jnp.bfloat16
ROWS, D = 80, 1152
PAIRS = 20480
SIDE = 16 * ROWS
BUNDLE = 4 * ROWS
HALF = 8 * ROWS
CUT = 48
SENDS, RECVS = 96, 96


def normalize(emb):
    full = emb.astype(F32)
    inverse = lax.rsqrt(jnp.sum(full * full, axis=1, keepdims=True) + 1e-06)
    return (full * inverse, inverse)


def back_norm(unit, inverse, direction):
    inner = jnp.sum(unit * direction, axis=1, keepdims=True)
    return inverse * (direction - unit * inner)


def at(slot, first=0, count=ROWS):
    return pl.ds(pl.multiple_of(slot * ROWS + first, 16), count)


class Links:
    def __init__(self, send, recv):
        self.send, self.recv = send, recv
        self.sent = []
        self.used = 0

    def ticket(self):
        self.used += 1
        return self.used - 1

    def start(self, src, dst, ticket, device):
        copy = pltpu.make_async_remote_copy(
            src_ref=src,
            dst_ref=dst,
            send_sem=self.send.at[len(self.sent)],
            recv_sem=self.recv.at[ticket],
            device_id=device,
            device_id_type=MESH,
        )
        copy.start()
        self.sent.append(copy)

    def arrived(self, dst, ticket):
        pltpu.make_async_copy(dst, dst, self.recv.at[ticket]).wait()

    def drain(self):
        for copy in self.sent:
            copy.wait_send()


def kernel(
    image_ref, text_ref, table_ref, log_scale_ref, bias_ref,
    loss_ref, grad_image_ref, grad_text_ref,
    imgs, txts, slopes, pimg, ptxt,
    mates, mate_rows, mate_cols, text_ids, loss_acc,
    b_far, b_near, a_far, a_near, sib, z_in,
    loss_x, loss_y, loss_z, loss_c,
    send_sems, recv_sems,
):
    img, txt = lax.axis_index("img"), lax.axis_index("txt")
    x, z_hi = img % 4, img // 4
    core, y, z_lo = txt % 2, (txt // 2) % 4, txt // 8
    z = z_hi * 4 + z_lo

    def dev(x, y, z, core):
        return {"img": (z // 4) * 4 + x, "txt": ((z % 4) * 4 + y) * 2 + core}

    def swap(a, b):
        return a + core * (b - a), b + core * (a - b)

    a, b = swap(x, y)

    def plane(a, b):
        px, py = swap(a % 4, b % 4)
        return dev(px, py, z, core)

    def along_z(k):
        return dev(x, y, (z + k) % 8, core)

    a_next, a_prev = plane(a + 1, b), plane(a + 3, b)
    b_next, b_prev = plane(a, b + 1), plane(a, b + 3)
    z_next, z_prev = along_z(1), along_z(7)
    sibling = dev(x, y, z, 1 - core)
    links = Links(send_sems, recv_sems)

    barrier = pltpu.get_barrier_semaphore()
    partners = [dev((x + k) % 4, y, z, core) for k in (1, 2, 3)]
    partners += [dev(x, (y + k) % 4, z, core) for k in (1, 2, 3)]
    partners += [along_z(k) for k in range(1, 8)] + [sibling]
    for device in partners:
        pl.semaphore_signal(barrier, inc=1, device_id=device, device_id_type=MESH)

    def img_slot(a, b):
        return (b % 4) * 4 + a % 4

    own = img_slot(a, b)
    own_text = core * 8 + z
    imgs[at(own), :] = normalize(image_ref[...])[0].astype(BF16)
    txts[at(own_text), :] = normalize(text_ref[...])[0].astype(BF16)
    mates[x] = table_ref[pl.ds(pl.multiple_of(z_lo * 8, 8), 8), :]
    pl.semaphore_wait(barrier, len(partners))

    def send_img(slot, ticket, device, first=0, count=ROWS):
        view = imgs.at[at(slot, first, count), :]
        links.start(view, view, ticket, device)

    def got_img(slot, ticket, first=0, count=ROWS):
        links.arrived(imgs.at[at(slot, first, count), :], ticket)

    def send_txt(slot, ticket, device, first=0, count=ROWS):
        view = txts.at[at(slot, first, count), :]
        links.start(view, view, ticket, device)

    def got_txt(slot, ticket, first=0, count=ROWS):
        links.arrived(txts.at[at(slot, first, count), :], ticket)

    ta = [links.ticket() for _ in range(4)]
    tb_next = [links.ticket() for _ in range(4)]
    tb_prev = [links.ticket() for _ in range(4)]
    tb_far = [links.ticket() for _ in range(4)]
    tz_next = [links.ticket() for _ in range(4)]
    tz_prev = [links.ticket() for _ in range(4)]
    t_sib = [links.ticket() for _ in range(8)]
    t_mates = [links.ticket() for _ in range(3)]

    order = [0, 3, 1, 2]

    def send_b(k):
        slot = img_slot(a + order[k], b)
        send_img(slot, tb_next[k], b_next)
        send_img(slot, tb_prev[k], b_prev)

    def forward_b(k):
        got_img(img_slot(a + order[k], b + 3), tb_next[k])
        got_img(img_slot(a + order[k], b + 1), tb_prev[k])
        if k % 2 == 0:
            send_img(img_slot(a + order[k], b + 3), tb_far[k], b_next)
        else:
            send_img(img_slot(a + order[k], b + 1), tb_far[k], b_prev)

    def z_slot(k):
        return core * 8 + (z + k) % 8

    def send_sib(k):
        send_txt(z_slot(k), t_sib[k], sibling)

    send_img(own, ta[0], a_next)
    send_img(own, ta[1], a_prev)
    send_txt(own_text, tz_next[0], z_next)
    send_txt(own_text, tz_prev[0], z_prev)
    send_b(0)
    for k in (1, 2, 3):
        links.start(mates.at[x], mates.at[x], t_mates[k - 1], partners[k - 1])
    send_sib(0)

    got_img(img_slot(a + 3, b), ta[0])
    send_img(img_slot(a + 3, b), ta[2], a_next, 0, CUT)
    got_img(img_slot(a + 1, b), ta[1])
    send_img(img_slot(a + 1, b), ta[3], a_prev, CUT, ROWS - CUT)
    for h in (1, 2, 3):
        last = h == 3
        got_txt(z_slot(-h), tz_next[h - 1])
        send_txt(z_slot(-h), tz_next[h], z_next, 0, CUT if last else ROWS)
        got_txt(z_slot(h), tz_prev[h - 1])
        if last:
            send_txt(z_slot(h), tz_prev[h], z_prev, CUT, ROWS - CUT)
        else:
            send_txt(z_slot(h), tz_prev[h], z_prev)
        send_sib(8 - h)
        send_sib(h)
        if h == 1:
            send_b(1)
            send_b(2)
            forward_b(0)
        if h == 2:
            got_img(img_slot(a + 2, b), ta[2], 0, CUT)
            got_img(img_slot(a + 2, b), ta[3], CUT, ROWS - CUT)
            send_b(3)
            forward_b(1)
            forward_b(2)
    got_txt(z_slot(4), tz_next[3], 0, CUT)
    got_txt(z_slot(4), tz_prev[3], CUT, ROWS - CUT)
    send_sib(4)
    forward_b(3)

    for k in (1, 2, 3):
        links.arrived(mates.at[(x + 4 - k) % 4], t_mates[k - 1])
    mate_rows[...] = jnp.zeros_like(mate_rows)
    for slot in range(16):
        px, py = swap(slot % 4, slot // 4)
        mate_rows[slot:slot + 1, :] = mates[px, pl.ds(2 * py + core, 1), :].astype(F32)
    turned = mate_rows[...].T
    for slot in range(16):
        mate_cols[slot * ROWS:(slot + 1) * ROWS, :] = jnp.broadcast_to(
            turned[0:ROWS, slot:slot + 1], (ROWS, 128)
        )
    column = lax.broadcasted_iota(jnp.int32, (8, SIDE), 1)
    ids = column
    for slot in range(16):
        c, pz = slot // 8, slot % 8
        start = ((((pz % 4) * 4 + y) * 2 + c) * 8 + (pz // 4) * 4 + x) * ROWS
        ids = jnp.where(column >= slot * ROWS, column - slot * ROWS + start, ids)
    text_ids[...] = ids.astype(F32)

    for k in range(8):
        got_txt((1 - core) * 8 + (z + k) % 8, t_sib[k])
    for k in range(4):
        got_img(img_slot(a + order[k], b + 2), tb_far[k])

    scale = jnp.exp(jnp.full((1, 1), log_scale_ref[0], F32))
    to_log2 = scale * math.log2(math.e)
    shift = jnp.full((1, 1), bias_ref[0] * math.log2(math.e), F32)
    loss_acc[...] = jnp.zeros_like(loss_acc)

    def tile(step, _):
        rows = pl.ds(pl.multiple_of((step // 5) * BUNDLE, BUNDLE), BUNDLE)
        cols = pl.ds(pl.multiple_of((step % 5) * 256, 256), 256)
        cosine = lax.dot_general(
            imgs[rows, :], txts[cols, :], (((1,), (1,)), ((), ())), preferred_element_type=F32
        )
        logits = cosine * to_log2 + shift
        e = jnp.exp2(logits)
        u = 1.0 + e
        r = 1.0 / u
        mate = mate_cols[rows, :]
        positive = jnp.concatenate([mate, mate], axis=1) == text_ids[0:1, cols]
        slopes[rows, cols] = jnp.where(positive, -r, e * r).astype(BF16)
        small = e < 0.015625
        series = e * (1.0 - e * (0.5 - e * (1.0 / 3.0 - e * 0.25)))
        factor = jnp.where(small, 1.0, u)
        term = jnp.where(small, series, 0.0) - jnp.where(positive, logits * math.log(2.0), 0.0)
        product = factor[0:80] * factor[80:160] * factor[160:240] * factor[240:320]
        total = jnp.log(product).reshape(10, 8, 256).sum(0) + term.reshape(40, 8, 256).sum(0)
        loss_acc[...] += total
        return 0

    lax.fori_loop(0, 20, tile, 0)

    lx = [links.ticket() for _ in range(3)]
    ly = [links.ticket() for _ in range(3)]
    lz = [links.ticket() for _ in range(7)]
    lc = links.ticket()

    def share(buffer, me, size, tickets, devices):
        for k in range(1, size):
            links.start(buffer.at[me], buffer.at[me], tickets[k - 1], devices[k - 1])

    def gathered(buffer, me, size, tickets):
        for k in range(1, size):
            links.arrived(buffer.at[(me + size - k) % size], tickets[k - 1])
        total = buffer[0]
        for k in range(1, size):
            total = total + buffer[k]
        return total

    part = jnp.sum(jnp.sum(loss_acc[...], axis=0, keepdims=True), axis=1, keepdims=True)
    loss_x[x] = jnp.broadcast_to(part, (8, 128))
    share(loss_x, x, 4, lx, partners[0:3])

    def image_part(bundle):
        rows = pl.ds(pl.multiple_of((bundle % 4) * BUNDLE, BUNDLE), BUNDLE)

        def chunk(n, _):
            cols = pl.ds(pl.multiple_of(n * 384, 384), 384)
            pimg[rows, cols] = jnp.dot(slopes[rows, :], txts[:, cols], preferred_element_type=F32)
            return 0

        lax.fori_loop(0, 3, chunk, 0)

    def text_part(half):
        rows = pl.ds(pl.multiple_of(half * HALF, 128), HALF)

        def chunk(n, _):
            cols = pl.ds(pl.multiple_of(n * 384, 384), 384)
            ptxt[rows, cols] = lax.dot_general(
                slopes[:, rows], imgs[:, cols], (((0,), (0,)), ((), ())), preferred_element_type=F32
            )
            return 0

        lax.fori_loop(0, 3, chunk, 0)

    def add(total, start, source, first, count):
        for k in range(0, count, 16):
            total[pl.ds(pl.multiple_of(start + k, 16), 16), :] += source[first + k:first + k + 16, :]

    ub_far = [links.ticket() for _ in range(2)]
    ub_near = [links.ticket() for _ in range(2)]
    ua_far = [links.ticket() for _ in range(2)]
    ua_near = [links.ticket() for _ in range(2)]
    uz = [[links.ticket() for _ in range(4)] for _ in range(2)]
    u_sib = links.ticket()

    def bundle_at(k, first=0, count=BUNDLE):
        return pl.ds(pl.multiple_of(((b + k) % 4) * BUNDLE + first, 16), count)

    image_part(b + 2)
    links.start(pimg.at[bundle_at(2, 0, 160), :], b_far.at[0], ub_far[0], b_next)
    links.start(pimg.at[bundle_at(2, 160, 160), :], b_far.at[1], ub_far[1], b_prev)
    text_part(1 - core)
    links.start(ptxt.at[pl.ds(pl.multiple_of((1 - core) * HALF, 16), HALF), :], sib, u_sib, sibling)
    loss_y[y] = gathered(loss_x, x, 4, lx)
    share(loss_y, y, 4, ly, partners[3:6])
    image_part(b + 1)
    links.arrived(b_far.at[0], ub_far[0])
    add(pimg, ((b + 1) % 4) * BUNDLE, b_far.at[0], 0, 160)
    links.start(pimg.at[bundle_at(1), :], b_near.at[0], ub_near[0], b_next)
    image_part(b + 3)
    links.arrived(b_far.at[1], ub_far[1])
    add(pimg, ((b + 3) % 4) * BUNDLE + 160, b_far.at[1], 0, 160)
    links.start(pimg.at[bundle_at(3), :], b_near.at[1], ub_near[1], b_prev)
    text_part(core)
    links.arrived(sib, u_sib)
    add(ptxt, core * HALF, sib, 0, HALF)

    def z_at(k, first=0, count=ROWS):
        return ptxt.at[at(core * 8 + (z + k) % 8, first, count), :]

    def z_start(k):
        return (core * 8 + (z + k) % 8) * ROWS

    rest = ROWS - CUT
    links.start(z_at(4, 0, CUT), z_in.at[0, 3, pl.ds(0, CUT), :], uz[0][3], z_next)
    links.start(z_at(4, CUT, rest), z_in.at[1, 3, pl.ds(0, rest), :], uz[1][3], z_prev)
    loss_z[z] = gathered(loss_y, y, 4, ly)
    share(loss_z, z, 8, lz, partners[6:13])
    image_part(b)

    links.arrived(z_in.at[0, 3, pl.ds(0, CUT), :], uz[0][3])
    add(ptxt, z_start(3), z_in.at[0, 3], 0, CUT)
    links.start(z_at(3), z_in.at[0, 2], uz[0][2], z_next)
    links.arrived(z_in.at[1, 3, pl.ds(0, rest), :], uz[1][3])
    add(ptxt, z_start(5) + CUT, z_in.at[1, 3], 0, rest)
    links.start(z_at(5), z_in.at[1, 2], uz[1][2], z_prev)

    def a_start(k):
        return img_slot(a + k, b) * ROWS

    links.arrived(b_near.at[0], ub_near[0])
    links.arrived(b_near.at[1], ub_near[1])

    def fold(k):
        start = a_start(k)
        offset = ((a + k) % 4) * ROWS
        for n in range(0, ROWS, 16):
            here = pl.ds(pl.multiple_of(start + n, 16), 16)
            there = pl.ds(pl.multiple_of(offset + n, 16), 16)
            pimg[here, :] += b_near[0, there, :] + b_near[1, there, :]

    fold(2)
    links.start(pimg.at[at(img_slot(a + 2, b), 0, CUT), :], a_far.at[0], ua_far[0], a_next)
    links.start(pimg.at[at(img_slot(a + 2, b), CUT, rest), :], a_far.at[1, pl.ds(0, rest), :], ua_far[1], a_prev)
    fold(1)
    fold(3)
    fold(0)

    for h in (2, 1):
        links.arrived(z_in.at[0, h], uz[0][h])
        add(ptxt, z_start(h), z_in.at[0, h], 0, ROWS)
        links.start(z_at(h), z_in.at[0, h - 1], uz[0][h - 1], z_next)
        links.arrived(z_in.at[1, h], uz[1][h])
        add(ptxt, z_start(8 - h), z_in.at[1, h], 0, ROWS)
        links.start(z_at(8 - h), z_in.at[1, h - 1], uz[1][h - 1], z_prev)
        if h == 2:
            links.arrived(a_far.at[0], ua_far[0])
            add(pimg, a_start(1), a_far.at[0], 0, CUT)
            links.start(pimg.at[at(img_slot(a + 1, b)), :], a_near.at[0], ua_near[0], a_next)
            links.arrived(a_far.at[1, pl.ds(0, rest), :], ua_far[1])
            add(pimg, a_start(3) + CUT, a_far.at[1], 0, rest)
            links.start(pimg.at[at(img_slot(a + 3, b)), :], a_near.at[1], ua_near[1], a_prev)

    loss_c[core] = gathered(loss_z, z, 8, lz)
    share(loss_c, core, 2, [lc], [sibling])
    links.arrived(a_near.at[0], ua_near[0])
    links.arrived(a_near.at[1], ua_near[1])
    image_sum = pimg[at(own), :] + a_near[0] + a_near[1]
    unit, inverse = normalize(image_ref[...])
    grad_image_ref[...] = back_norm(unit, inverse, scale * image_sum)

    links.arrived(z_in.at[0, 0], uz[0][0])
    links.arrived(z_in.at[1, 0], uz[1][0])
    text_sum = ptxt[at(own_text), :] + z_in[0, 0] + z_in[1, 0]
    unit, inverse = normalize(text_ref[...])
    grad_text_ref[...] = back_norm(unit, inverse, scale * text_sum)
    loss_ref[...] = gathered(loss_c, core, 2, [lc]) * (1.0 / PAIRS)
    links.drain()


def on_device(image_emb, text_emb, partner, log_scale, bias):
    table = jnp.pad(partner.reshape(32, ROWS), ((0, 0), (0, 128 - ROWS)))
    vmem, smem = pl.BlockSpec(memory_space=pltpu.VMEM), pl.BlockSpec(memory_space=pltpu.SMEM)
    loss, grad_image, grad_text = pl.pallas_call(
        kernel,
        out_shape=(
            jax.ShapeDtypeStruct((8, 128), F32),
            jax.ShapeDtypeStruct((ROWS, D), F32),
            jax.ShapeDtypeStruct((ROWS, D), F32),
        ),
        in_specs=[vmem, vmem, vmem, smem, smem],
        out_specs=(vmem, vmem, vmem),
        scratch_shapes=[
            pltpu.VMEM((SIDE, D), BF16),
            pltpu.VMEM((SIDE, D), BF16),
            pltpu.VMEM((SIDE, SIDE), BF16),
            pltpu.VMEM((SIDE, D), F32),
            pltpu.VMEM((SIDE, D), F32),
            pltpu.VMEM((4, 8, 128), jnp.int32),
            pltpu.VMEM((128, 128), F32),
            pltpu.VMEM((SIDE, 128), F32),
            pltpu.VMEM((8, SIDE), F32),
            pltpu.VMEM((8, 256), F32),
            pltpu.VMEM((2, 160, D), F32),
            pltpu.VMEM((2, BUNDLE, D), F32),
            pltpu.VMEM((2, CUT, D), F32),
            pltpu.VMEM((2, ROWS, D), F32),
            pltpu.VMEM((HALF, D), F32),
            pltpu.VMEM((2, 4, ROWS, D), F32),
            pltpu.VMEM((4, 8, 128), F32),
            pltpu.VMEM((4, 8, 128), F32),
            pltpu.VMEM((8, 8, 128), F32),
            pltpu.VMEM((2, 8, 128), F32),
            pltpu.SemaphoreType.DMA((SENDS,)),
            pltpu.SemaphoreType.DMA((RECVS,)),
        ],
        compiler_params=pltpu.CompilerParams(
            collective_id=0, has_side_effects=True, vmem_limit_bytes=60 * 1024 * 1024
        ),
    )(image_emb, text_emb, table, log_scale, bias)
    return (loss[0, 0:1], grad_image, grad_text)


def solution(mesh):
    return jax.shard_map(
        on_device,
        mesh=mesh,
        in_specs=(P(("img", "txt"), None), P(("txt", "img"), None), P("img"), P(), P()),
        out_specs=(P(), P(("img", "txt"), None), P(("txt", "img"), None)),
        check_vma=False,
    )
```

time: 448 us -> 112 us (0.25)
  the two profiles are of different devices: /device:TPU:1 before, /device:TPU:8 now
where the time goes in v1:
time: 112 us; the launch traced here: 111 us
  Pallas kernels  104 us (93%)
  local copies, waits for them, and re-layouts  5.12 us (5%)
  between operations  1.93 us (2%)
    pallas_call x1, Pallas kernels, on_device(): pl.pallas_call(kernel, out_shape=(jax.ShapeDtypeStruct((8, 128), F32), ja...  104 us
    unnamed x4, local copies, waits for them, and re-layouts  2.54 us

profile of v1, /device:TPU:8, one launch (start us, length us, event | category | flops | bytes accessed | tf_op | source)
XLA Modules:
  0.0 111.3 jit_solution(11374354120854834912)
XLA Ops:
  1.9 0.8 reshape.9
  2.7 0.6 pad.4.table_ref
  3.3 104.3 %shard_map.76 = (f32[8,128]{1,0:T(8,128)}, f32[80,1152]{1,0:T(8,128)}, f32[80,1152]{1,0:T(8,128)}) custom-call(bf16[80,1152]{1,0:T(8,128)(2,1)} %image_ref.1, bf16[80,1152]{1,0:T(8,128)(2,1)} %text_ref.1, s32[32,128]{1,0:T(8,128)} %pad.4.table_ref, f32[1]{0:T(128)S(6)} %copy.10.log_scale_ref, f32[1]{0:T(128)S(6)} %copy.11.bias_ref), custom_call_target="tpu_custom_call" | custom-call | tf_op jit(solution)/shard_map/pallas_call | solution.py:407
  107.6 1.2 %slice.3 = f32[1,1]{1,0:T(1,128)} slice(f32[8,128]{1,0:T(8,128)} %get-tuple-element.6), slice={[0:1], [0:1]} | slice | bytes 8 | tf_op jit(solution)/shard_map/slice | solution.py:444
  108.8 0.0 copy-start
  108.8 1.8 %copy.12 = f32[80,1152]{1,0:T(8,128)} copy(f32[80,1152]{1,0:T(8,128)} %get-tuple-element.13) | data formatting | bytes 737280
  110.6 0.0 copy-done
  110.6 0.7 copy.13
Async XLA Ops:
  108.8 1.8 %copy-start = (f32[80,1152]{1,0:T(8,128)S(1)}, f32[80,1152]{1,0:T(8,128)}, u32[]{:S(2)}) copy-start(f32[80,1152]{1,0:T(8,128)} %get-tuple-element.14) | copy-start | bytes 1105924

commit v2 on v0

v2 whole, which is shorter than its diff:
```python
import math

import jax
import jax.numpy as jnp
from jax import lax
from jax.experimental import pallas as pl
from jax.experimental.pallas import tpu as pltpu
from jax.sharding import PartitionSpec as P

MESH = pl.DeviceIdType.MESH
F32, BF16, I16 = jnp.float32, jnp.bfloat16, jnp.int16
ROWS, D = 80, 1152
PAIRS = 20480
SIDE = 16 * ROWS
BUNDLE = 4 * ROWS
OFF4 = (0, 1, 3, 2)
OFF8 = (0, 1, 7, 2, 6, 3, 5, 4)
KEY4 = {off: k for k, off in enumerate(OFF4)}
KEY8 = {off: k for k, off in enumerate(OFF8)}
PIECES = ((0, 32), (32, 16), (48, 32))
FULL = ((0, 1), (2,))
COUNT = 224


def normalize(emb):
    full = emb.astype(F32)
    inverse = lax.rsqrt(jnp.sum(full * full, axis=1, keepdims=True) + 1e-06)
    return (full * inverse, inverse)


def back_norm(unit, inverse, direction):
    inner = jnp.sum(unit * direction, axis=1, keepdims=True)
    return inverse * (direction - unit * inner)


class Links:
    def __init__(self, send, recv):
        self.send, self.recv = send, recv
        self.sent = []
        self.used = 0

    def tickets(self, count):
        self.used += count
        assert self.used <= COUNT
        return list(range(self.used - count, self.used))

    def start(self, src, dst, ticket, device):
        copy = pltpu.make_async_remote_copy(
            src_ref=src,
            dst_ref=dst,
            send_sem=self.send.at[len(self.sent)],
            recv_sem=self.recv.at[ticket],
            device_id=device,
            device_id_type=MESH,
        )
        copy.start()
        self.sent.append(copy)

    def arrived(self, dst, ticket):
        pltpu.make_async_copy(dst, dst, self.recv.at[ticket]).wait()

    def drain(self):
        for copy in self.sent:
            copy.wait_send()


def by_lanes(body):
    def step(n, _):
        for k in range(3):
            body(pl.ds(pl.multiple_of((n * 3 + k) * 128, 128), 128))
        return 0

    lax.fori_loop(0, D // 384, step, 0)


def widen(q, s, rows, lanes):
    return q[rows, lanes].astype(F32) * s[:, lanes]


def narrow(value, q, s, rows):
    def body(lanes):
        v = value(lanes)
        top = jnp.maximum(jnp.max(jnp.abs(v), axis=0, keepdims=True), 1e-30)
        q[rows, lanes] = jnp.round(v * (32767.0 * pltpu.reciprocal(top, approx=True))).astype(I16)
        s[:, lanes] = top * (1.0 / 32767.0)

    by_lanes(body)


def kernel(
    image_ref, text_ref, table_ref, log_scale_ref, bias_ref,
    loss_ref, grad_image_ref, grad_text_ref,
    imgs, txts, slopes, pimg, ptxt,
    mates, mate_rows, mate_all, mate_cols, text_ids, loss_acc,
    far_q, far_s, far_qi, far_si,
    near_q, near_s, near_qi, near_si,
    a_q, a_s, a_qi, a_si,
    sib_q, sib_s, sib_qi, sib_si,
    z_q, z_s, z_qi, z_si,
    loss_x, loss_y, loss_z, loss_c,
    send_sems, recv_sems,
):
    img, txt = lax.axis_index("img"), lax.axis_index("txt")
    x, z_hi = img % 4, img // 4
    core, y, z_lo = txt % 2, (txt // 2) % 4, txt // 8
    z = z_hi * 4 + z_lo

    def dev(x, y, z, core):
        return {"img": (z // 4) * 4 + x, "txt": ((z % 4) * 4 + y) * 2 + core}

    def swap(a, b):
        return a + core * (b - a), b + core * (a - b)

    a, b = swap(x, y)

    def plane(a, b):
        px, py = swap(a % 4, b % 4)
        return dev(px, py, z, core)

    def along_z(k):
        return dev(x, y, (z + k) % 8, core)

    to_a = [plane(a + off, b) for off in OFF4]
    to_b = (plane(a, b + 1), plane(a, b + 3))
    to_z = (along_z(1), along_z(7))
    sibling = dev(x, y, z, 1 - core)
    links = Links(send_sems, recv_sems)

    barrier = pltpu.get_barrier_semaphore()
    partners = [dev((x + k) % 4, y, z, core) for k in (1, 2, 3)]
    partners += [dev(x, (y + k) % 4, z, core) for k in (1, 2, 3)]
    partners += [along_z(k) for k in range(1, 8)] + [sibling]
    for device in partners:
        pl.semaphore_signal(barrier, inc=1, device_id=device, device_id_type=MESH)

    imgs[0:ROWS, :] = normalize(image_ref[...])[0].astype(BF16)
    txts[0:ROWS, :] = normalize(text_ref[...])[0].astype(BF16)
    for k in range(5):
        mates[x, k:k + 1, :] = table_ref[pl.ds(z_lo * 5 + k, 1), :]
    loss_acc[...] = jnp.zeros_like(loss_acc)
    pl.semaphore_wait(barrier, len(partners))

    def img_at(kb, ka):
        return imgs.at[pl.ds((kb * 4 + ka) * ROWS, ROWS), :]

    def txt_at(kz, cc, first=0, count=ROWS):
        return txts.at[pl.ds((kz * 2 + cc) * ROWS + first, count), :]

    ta = links.tickets(4)
    tb = [links.tickets(4) for _ in range(2)]
    tb_far = links.tickets(4)
    tz = [[links.tickets(3) for _ in range(4)] for _ in range(2)]
    t_sib = links.tickets(8)
    t_mates = links.tickets(3)

    def b_key(direction):
        return KEY4[3 if direction == 0 else 1]

    def z_key(direction, h):
        return KEY8[-h % 8 if direction == 0 else h]

    def send_b(ka):
        for d in (0, 1):
            links.start(img_at(0, ka), img_at(b_key(d), ka), tb[d][ka], to_b[d])

    def got_b(ka):
        for d in (0, 1):
            links.arrived(img_at(b_key(d), ka), tb[d][ka])
            if ka % 2 == d:
                links.start(img_at(b_key(d), ka), img_at(3, ka), tb_far[ka], to_b[d])

    def send_z(d, h, p):
        first, count = PIECES[p]
        links.start(
            txt_at(z_key(d, h - 1) if h > 1 else 0, 0, first, count),
            txt_at(z_key(d, h), 0, first, count),
            tz[d][h - 1][p],
            to_z[d],
        )

    def got_z(h):
        for p in (0, 2, 1):
            for d in (0, 1):
                if h == 4 and p not in FULL[d]:
                    continue
                first, count = PIECES[p]
                links.arrived(txt_at(z_key(d, h), 0, first, count), tz[d][h - 1][p])
                if h < 3 or (h == 3 and p in FULL[d]):
                    send_z(d, h + 1, p)

    def send_sib(kz):
        links.start(txt_at(kz, 0), txt_at(kz, 1), t_sib[kz], sibling)

    def got_sib(kz):
        links.arrived(txt_at(kz, 1), t_sib[kz])

    for p in (0, 2, 1):
        for d in (0, 1):
            send_z(d, 1, p)
    for ka in (3, 1, 2):
        off = OFF4[ka]
        links.start(img_at(0, 0), img_at(0, KEY4[-off % 4]), ta[ka], to_a[ka])
    send_b(0)
    send_sib(0)
    for k in (1, 2, 3):
        links.start(mates.at[x], mates.at[x], t_mates[k - 1], partners[k - 1])

    column = lax.broadcasted_iota(jnp.int32, (8, SIDE), 1)
    ids = column
    for kz in range(8):
        for cc in (0, 1):
            slot, pz = kz * 2 + cc, (z + OFF8[kz]) % 8
            c = core if cc == 0 else 1 - core
            start = ((((pz % 4) * 4 + y) * 2 + c) * 8 + (pz // 4) * 4 + x) * ROWS
            ids = jnp.where(column >= slot * ROWS, column - slot * ROWS + start, ids)
    text_ids[...] = ids.astype(F32)

    got_z(1)
    send_sib(1)
    send_sib(2)
    for ka in (1, 2, 3):
        links.arrived(img_at(0, KEY4[-OFF4[ka] % 4]), ta[ka])
        send_b(KEY4[-OFF4[ka] % 4])
    got_b(0)

    for k in (1, 2, 3):
        links.arrived(mates.at[(x + 4 - k) % 4], t_mates[k - 1])
    mate_rows[...] = jnp.zeros_like(mate_rows)
    for px in range(4):
        mate_rows[px * 8:px * 8 + 5, :] = mates[px, 0:5, :].astype(F32)
    turned = mate_rows[...].T
    for px in range(4):
        for k in range(5):
            mate_all[px, k * 128:(k + 1) * 128, :] = jnp.broadcast_to(
                turned[:, px * 8 + k:px * 8 + k + 1], (128, 128)
            )
    for kb in range(4):
        for ka in range(4):
            px, py = swap((a + OFF4[ka]) % 4, (b + OFF4[kb]) % 4)
            start = pl.multiple_of((2 * py + core) * ROWS, 16)
            mate_cols[(kb * 4 + ka) * ROWS:(kb * 4 + ka + 1) * ROWS, :] = mate_all[px, pl.ds(start, ROWS), :]

    scale = jnp.exp(jnp.full((1, 1), log_scale_ref[0], F32))
    to_log2 = scale * math.log2(math.e)
    shift = jnp.full((1, 1), bias_ref[0] * math.log2(math.e), F32)

    def tile(kb, first, count):
        rows = pl.ds(kb * BUNDLE if isinstance(kb, int) else pl.multiple_of(kb * BUNDLE, BUNDLE), BUNDLE)
        cols = pl.ds(first, count)
        cosine = lax.dot_general(
            imgs[rows, :], txts[cols, :], (((1,), (1,)), ((), ())), preferred_element_type=F32
        )
        logits = cosine * to_log2 + shift
        e = jnp.exp2(logits)
        u = 1.0 + e
        r = pltpu.reciprocal(u, approx=True)
        mate = mate_cols[rows, :]
        positive = jnp.concatenate([mate] * (count // 128), axis=1) == text_ids[0:1, cols]
        slopes[rows, cols] = jnp.where(positive, -r, e * r).astype(BF16)
        lost = (e - (u - 1.0)) * r
        paired = jnp.where(positive, logits, 0.0)
        product = u[0:80] * u[80:160] * u[160:240] * u[240:320]
        total = jnp.log(product).reshape(10, 8, count).sum(0)
        total += lost.reshape(40, 8, count).sum(0) - paired.reshape(40, 8, count).sum(0) * math.log(2.0)
        folded = total[:, 0:128]
        for k in range(128, count, 128):
            folded = folded + total[:, k:k + 128]
        loss_acc[...] += folded

    def tiles(low, high, first, count):
        def step(kb, _):
            tile(kb, first, count)
            return 0

        lax.fori_loop(low, high, step, 0)

    got_sib(0)
    got_sib(1)
    tile(0, 0, 256)
    got_z(2)
    send_sib(3)
    send_sib(4)
    got_b(1)
    got_b(2)
    got_sib(2)
    got_sib(3)
    got_sib(4)
    tile(0, 256, 512)
    got_z(3)
    send_sib(5)
    send_sib(6)
    got_b(3)
    tiles(1, 3, 0, 768)
    got_z(4)
    send_sib(7)
    got_sib(5)
    got_sib(6)
    got_sib(7)
    tiles(0, 3, 768, 512)
    for ka in range(4):
        links.arrived(img_at(3, ka), tb_far[ka])
    tile(3, 0, 1280)

    lx, ly, lz, lc = links.tickets(3), links.tickets(3), links.tickets(7), links.tickets(1)

    def share(buffer, me, size, tickets, devices):
        for k in range(1, size):
            links.start(buffer.at[me], buffer.at[me], tickets[k - 1], devices[k - 1])

    def gathered(buffer, me, size, tickets):
        for k in range(1, size):
            links.arrived(buffer.at[(me + size - k) % size], tickets[k - 1])
        total = buffer[0]
        for k in range(1, size):
            total = total + buffer[k]
        return total

    def image_part(kb):
        rows = pl.ds(kb * BUNDLE, BUNDLE)
        pimg[rows, :] = jnp.dot(slopes[rows, :], txts[...], preferred_element_type=F32)

    def text_part(first, count):
        rows = pl.ds(first, count)
        ptxt[rows, :] = lax.dot_general(
            slopes[:, rows], imgs[...], (((0,), (0,)), ((), ())), preferred_element_type=F32
        )

    whole = pl.ds(0, ROWS)

    def send_pair(q, s, q_in, s_in, tickets, device):
        links.start(q, q_in, tickets[0], device)
        links.start(s, s_in, tickets[1], device)

    def got_pair(q_in, s_in, tickets):
        links.arrived(q_in, tickets[0])
        links.arrived(s_in, tickets[1])

    def img_rows(kb, ka):
        return pl.ds((kb * 4 + ka) * ROWS, ROWS)

    FAR = ((3, 2), (1, 0))
    u_far = {ka: links.tickets(2) for ka in range(4)}
    u_near = [{ka: links.tickets(2) for ka in range(4)} for _ in range(2)]
    u_a = {ka: links.tickets(2) for ka in (1, 2, 3)}
    u_sib = [links.tickets(2) for _ in range(8)]
    u_z = [[[links.tickets(2) for _ in range(3)] for _ in range(4)] for _ in range(2)]

    def send_far():
        for n in (0, 1):
            for d in (0, 1):
                ka = FAR[d][n]
                narrow(lambda lanes: pimg[img_rows(3, ka), lanes], far_q.at[ka], far_s.at[ka], whole)
                send_pair(far_q.at[ka], far_s.at[ka], far_qi.at[ka], far_si.at[ka], u_far[ka], to_b[d])

    def send_near(d, ka):
        kb = KEY4[1 if d == 0 else 3]
        added = ka in FAR[d]
        if added:
            got_pair(far_qi.at[ka], far_si.at[ka], u_far[ka])

        def value(lanes):
            v = pimg[img_rows(kb, ka), lanes]
            return v + widen(far_qi.at[ka], far_si.at[ka], whole, lanes) if added else v

        n = d * 4 + ka
        narrow(value, near_q.at[n], near_s.at[n], whole)
        send_pair(near_q.at[n], near_s.at[n], near_qi.at[n], near_si.at[n], u_near[d][ka], to_b[d])

    def fold(ka):
        for d in (0, 1):
            got_pair(near_qi.at[d * 4 + ka], near_si.at[d * 4 + ka], u_near[d][ka])

        def value(lanes):
            v = pimg[img_rows(0, ka), lanes]
            return v + widen(near_qi.at[ka], near_si.at[ka], whole, lanes) + widen(
                near_qi.at[4 + ka], near_si.at[4 + ka], whole, lanes
            )

        if ka:
            narrow(value, a_q.at[ka], a_s.at[ka], whole)
            send_pair(a_q.at[ka], a_s.at[ka], a_qi.at[ka], a_si.at[ka], u_a[ka], to_a[ka])
        else:
            def body(lanes):
                pimg[0:ROWS, lanes] = value(lanes)

            by_lanes(body)

    def swap_text(kz):
        rows = pl.ds((kz * 2 + 1) * ROWS, ROWS)
        narrow(lambda lanes: ptxt[rows, lanes], sib_q.at[kz], sib_s.at[kz], whole)
        send_pair(sib_q.at[kz], sib_s.at[kz], sib_qi.at[kz], sib_si.at[kz], u_sib[kz], sibling)

    def got_swap(kz):
        got_pair(sib_qi.at[kz], sib_si.at[kz], u_sib[kz])

    def z_piece(buffer, d, r, p):
        return buffer.at[d * 4 + r - 1, pl.ds(*PIECES[p]), :]

    def z_step(d, r, p):
        return (d * 4 + r - 1) * 3 + p

    def got_zsum(d, r, p):
        got_pair(z_piece(z_qi, d, r, p), z_si.at[z_step(d, r, p)], u_z[d][r - 1][p])

    def send_zsum(d, r, p):
        first, count = PIECES[p]
        kz = KEY8[r % 8 if d == 0 else -r % 8]
        added = r < 3 or (r == 3 and p in FULL[d])
        if added:
            got_zsum(d, r + 1, p)
        here = pl.ds(first, count)

        def value(lanes):
            v = ptxt[pl.ds(kz * 2 * ROWS + first, count), lanes] + widen(sib_qi.at[kz], sib_si.at[kz], here, lanes)
            if added:
                v = v + widen(z_qi.at[d * 4 + r], z_si.at[z_step(d, r + 1, p)], here, lanes)
            return v

        n = z_step(d, r, p)
        narrow(value, z_q.at[d * 4 + r - 1], z_s.at[n], here)
        send_pair(
            z_piece(z_q, d, r, p), z_s.at[n], z_piece(z_qi, d, r, p), z_si.at[n], u_z[d][r - 1][p], to_z[d]
        )

    image_part(3)
    send_far()
    part = jnp.sum(jnp.sum(loss_acc[...], axis=0, keepdims=True), axis=1, keepdims=True)
    loss_x[x] = jnp.broadcast_to(part, (8, 128))
    share(loss_x, x, 4, lx, partners[0:3])
    text_part(768, 512)
    for kz in (7, 5, 6):
        swap_text(kz)
    image_part(1)
    image_part(2)
    send_near(0, 1)
    send_near(1, 3)
    got_swap(7)
    for p, d in ((0, 0), (2, 1), (1, 0)):
        send_zsum(d, 4, p)
    got_swap(5)
    got_swap(6)
    for p, d in ((2, 0), (0, 1), (1, 1)):
        send_zsum(d, 3, p)
    send_near(0, 3)
    send_near(1, 1)
    send_near(0, 0)
    send_near(1, 2)
    text_part(256, 512)
    for kz in (3, 4, 2):
        swap_text(kz)
    loss_y[y] = gathered(loss_x, x, 4, lx)
    share(loss_y, y, 4, ly, partners[3:6])
    send_near(0, 2)
    send_near(1, 0)
    for p, d in ((0, 0), (2, 1), (1, 0)):
        send_zsum(d, 3, p)
    text_part(0, 256)
    for kz in (1, 0):
        swap_text(kz)
    image_part(0)
    loss_z[z] = gathered(loss_y, y, 4, ly)
    share(loss_z, z, 8, lz, partners[6:13])
    got_swap(3)
    got_swap(4)
    for p, d in ((2, 0), (0, 1), (1, 1), (0, 0), (2, 1), (1, 0)):
        send_zsum(d, 2, p)
    fold(3)
    fold(1)
    got_swap(1)
    got_swap(2)
    for p, d in ((2, 0), (0, 1), (1, 1), (0, 0), (2, 1), (1, 0)):
        send_zsum(d, 1, p)
    fold(2)
    fold(0)
    loss_c[core] = gathered(loss_z, z, 8, lz)
    share(loss_c, core, 2, lc, [sibling])
    got_swap(0)

    for ka in (1, 2, 3):
        got_pair(a_qi.at[ka], a_si.at[ka], u_a[ka])

    def image_sum(lanes):
        v = pimg[0:ROWS, lanes]
        for ka in (1, 2, 3):
            v = v + widen(a_qi.at[ka], a_si.at[ka], whole, lanes)
        pimg[0:ROWS, lanes] = v

    by_lanes(image_sum)
    unit, inverse = normalize(image_ref[...])
    grad_image_ref[...] = back_norm(unit, inverse, scale * pimg[0:ROWS, :])

    for p, d in ((2, 0), (0, 1), (1, 1), (0, 0), (2, 1), (1, 0)):
        got_zsum(d, 1, p)

    def text_sum(lanes):
        for p, (first, count) in enumerate(PIECES):
            here = pl.ds(first, count)
            v = ptxt[here, lanes] + widen(sib_qi.at[0], sib_si.at[0], here, lanes)
            for d in (0, 1):
                v = v + widen(z_qi.at[d * 4], z_si.at[z_step(d, 1, p)], here, lanes)
            ptxt[here, lanes] = v

    by_lanes(text_sum)
    unit, inverse = normalize(text_ref[...])
    grad_text_ref[...] = back_norm(unit, inverse, scale * ptxt[0:ROWS, :])
    loss_ref[...] = gathered(loss_c, core, 2, lc) * (1.0 / PAIRS)
    links.drain()


def on_device(image_emb, text_emb, partner, log_scale, bias):
    vmem, smem = pl.BlockSpec(memory_space=pltpu.VMEM), pl.BlockSpec(memory_space=pltpu.SMEM)

    def messages(count):
        return [pltpu.VMEM((count, ROWS, D), I16), pltpu.VMEM((count, 1, D), F32)] * 2

    loss, grad_image, grad_text = pl.pallas_call(
        kernel,
        out_shape=(
            jax.ShapeDtypeStruct((8, 128), F32),
            jax.ShapeDtypeStruct((ROWS, D), F32),
            jax.ShapeDtypeStruct((ROWS, D), F32),
        ),
        in_specs=[vmem, vmem, vmem, smem, smem],
        out_specs=(vmem, vmem, vmem),
        scratch_shapes=[
            pltpu.VMEM((SIDE, D), BF16),
            pltpu.VMEM((SIDE, D), BF16),
            pltpu.VMEM((SIDE, SIDE), BF16),
            pltpu.VMEM((SIDE, D), F32),
            pltpu.VMEM((SIDE, D), F32),
            pltpu.VMEM((4, 8, 128), jnp.int32),
            pltpu.VMEM((128, 128), F32),
            pltpu.VMEM((4, 640, 128), F32),
            pltpu.VMEM((SIDE, 128), F32),
            pltpu.VMEM((8, SIDE), F32),
            pltpu.VMEM((8, 128), F32),
            *messages(4),
            *messages(8),
            *messages(4),
            *messages(8),
            *[pltpu.VMEM((8, ROWS, D), I16), pltpu.VMEM((24, 1, D), F32)] * 2,
            pltpu.VMEM((4, 8, 128), F32),
            pltpu.VMEM((4, 8, 128), F32),
            pltpu.VMEM((8, 8, 128), F32),
            pltpu.VMEM((2, 8, 128), F32),
            pltpu.SemaphoreType.DMA((COUNT,)),
            pltpu.SemaphoreType.DMA((COUNT,)),
        ],
        compiler_params=pltpu.CompilerParams(
            collective_id=0, has_side_effects=True, vmem_limit_bytes=60 * 1024 * 1024
        ),
    )(image_emb, text_emb, partner.reshape(20, 128), log_scale, bias)
    return (loss[0, 0:1], grad_image, grad_text)


def solution(mesh):
    return jax.shard_map(
        on_device,
        mesh=mesh,
        in_specs=(P(("img", "txt"), None), P(("txt", "img"), None), P("img"), P(), P()),
        out_specs=(P(), P(("img", "txt"), None), P(("txt", "img"), None)),
        check_vma=False,
    )
```

time: 448 us -> 76.6 us (0.17); the launches traced: 443 us -> 76.4 us
  waiting for transfers between devices: 299 us -> 0 us
  blocking collectives: 84.3 us -> 0 us
  Pallas kernels: 0 us -> 70.8 us
  matrix products: 28.6 us -> 0 us
  between operations: 16.9 us -> 1.93 us
  other arithmetic: 11.7 us -> 0 us
    reduce_scatter x2 -> x0, waiting for transfers between devices: 166 us -> none  [the longest x1 155 us: on_device(): lax.psum_scatter(image_part, 'txt', scatter_dimension=0, tiled=True)]
    all_gather x2 -> x0, waiting for transfers between devices: 133 us -> none  [the longest x1 67.1 us: on_device(): texts = lax.all_gather(text_wire, 'img', axis=0, tiled=True)]
    psum x1 -> x0, blocking collectives: 84.3 us -> none  [on_device(): loss_total = lax.psum(part_loss, ('img', 'txt'))]
    pallas_call x0 -> x1, Pallas kernels: none -> 70.8 us  [on_device(): pl.pallas_call(kernel, out_shape=(jax.ShapeDtypeStruct((8, 128), F32), ja...]
    dot_general x3 -> x0, matrix products: 28.6 us -> none  [the longest x1 13.1 us: on_device(): jnp.einsum('pd,qd->pq', piece, texts, preferred_element_type=jnp.float32)]
    reduce_sum x4 -> x0, other arithmetic: 4.53 us -> none  [the longest x2 2.42 us: back_norm(): inner = jnp.sum(unit * direction, axis=1, keepdims=True)]
  transfers between devices with their start and end apart: 4 -> 0, of which waited for: 4 -> 0; matrix products, arithmetic and copies ran while one was open for 3% -> 0% of each run, Pallas kernels for 0% -> 0%
where the time goes in v2:
time: 76.6 us; the launch traced here: 76.4 us
  Pallas kernels  70.8 us (92%)
  local copies, waits for them, and re-layouts  3.73 us (5%)
  between operations  1.93 us (3%)
    pallas_call x1, Pallas kernels, on_device(): pl.pallas_call(kernel, out_shape=(jax.ShapeDtypeStruct((8, 128), F32), ja...  70.8 us
    unnamed x4, local copies, waits for them, and re-layouts  2.54 us

profile of v2, /device:TPU:1, one launch (start us, length us, event | category | flops | bytes accessed | tf_op | source)
XLA Modules:
  0.0 76.4 jit_solution(8750084063331827730)
XLA Ops:
  1.9 70.8 %shard_map.76 = (f32[8,128]{1,0:T(8,128)}, f32[80,1152]{1,0:T(8,128)}, f32[80,1152]{1,0:T(8,128)}) custom-call(bf16[80,1152]{1,0:T(8,128)(2,1)} %image_ref.1, bf16[80,1152]{1,0:T(8,128)(2,1)} %text_ref.1, s32[20,128]{1,0:T(8,128)} %bitcast.2, f32[1]{0:T(128)S(6)} %copy.10.log_scale_ref, f32[1]{0:T(128)S(6)} %copy.11.bias_ref), custom_call_target="tpu_custom_call" | custom-call | tf_op jit(solution)/shard_map/pallas_call | solution.py:516
  72.7 1.2 %slice.3 = f32[1,1]{1,0:T(1,128)} slice(f32[8,128]{1,0:T(8,128)} %get-tuple-element.6), slice={[0:1], [0:1]} | slice | bytes 8 | tf_op jit(solution)/shard_map/slice | solution.py:553
  73.9 0.0 copy-start
  73.9 1.8 %copy.12 = f32[80,1152]{1,0:T(8,128)} copy(f32[80,1152]{1,0:T(8,128)} %get-tuple-element.13) | data formatting | bytes 737280
  75.7 0.0 copy-done
  75.7 0.7 copy.13
Async XLA Ops:
  73.9 1.8 %copy-start = (f32[80,1152]{1,0:T(8,128)S(1)}, f32[80,1152]{1,0:T(8,128)}, u32[]{:S(2)}) copy-start(f32[80,1152]{1,0:T(8,128)} %get-tuple-element.14) | copy-start | bytes 1105924

commit v3 on v2

--- a/solution.py
+++ b/solution.py
@@ -19,6 +19,8 @@
 KEY8 = {off: k for k, off in enumerate(OFF8)}
 PIECES = ((0, 32), (32, 16), (48, 32))
 FULL = ((0, 1), (2,))
+CUT = ((0, 48), (48, 32))
+FAR_PARTS = (((0, 32), (32, 48)), (None, (0, 80)), ((0, 80), None), CUT)
 COUNT = 224
 
 
@@ -36,7 +38,7 @@
 class Links:
     def __init__(self, send, recv):
         self.send, self.recv = send, recv
-        self.sent = []
+        self.sent, self.open = [], []
         self.used = 0
 
     def tickets(self, count):
@@ -55,13 +57,15 @@
         )
         copy.start()
         self.sent.append(copy)
+        self.open.append(copy)
 
     def arrived(self, dst, ticket):
         pltpu.make_async_copy(dst, dst, self.recv.at[ticket]).wait()
 
     def drain(self):
-        for copy in self.sent:
+        for copy in self.open:
             copy.wait_send()
+        self.open = []
 
 
 def by_lanes(body):
@@ -87,9 +91,19 @@
     by_lanes(body)
 
 
+def finish(image_ref, text_ref, loss_part_ref, image_dir_ref, text_dir_ref, loss_ref, grad_image_ref, grad_text_ref):
+    loss_ref[...] = loss_part_ref[0:1, 0:1]
+    for emb_ref, dir_ref, grad_ref in (
+        (image_ref, image_dir_ref, grad_image_ref),
+        (text_ref, text_dir_ref, grad_text_ref),
+    ):
+        unit, inverse = normalize(emb_ref[...])
+        grad_ref[...] = back_norm(unit, inverse, dir_ref[...])
+
+
 def kernel(
     image_ref, text_ref, table_ref, log_scale_ref, bias_ref,
-    loss_ref, grad_image_ref, grad_text_ref,
+    loss_ref, image_dir_ref, text_dir_ref,
     imgs, txts, slopes, pimg, ptxt,
     mates, mate_rows, mate_all, mate_cols, text_ids, loss_acc,
     far_q, far_s, far_qi, far_si,
@@ -146,9 +160,9 @@
     def txt_at(kz, cc, first=0, count=ROWS):
         return txts.at[pl.ds((kz * 2 + cc) * ROWS + first, count), :]
 
-    ta = links.tickets(4)
+    ta, ta_far = links.tickets(2), links.tickets(2)
     tb = [links.tickets(4) for _ in range(2)]
-    tb_far = links.tickets(4)
+    tb_far = [links.tickets(2) for _ in range(4)]
     tz = [[links.tickets(3) for _ in range(4)] for _ in range(2)]
     t_sib = links.tickets(8)
     t_mates = links.tickets(3)
@@ -159,6 +173,22 @@
     def z_key(direction, h):
         return KEY8[-h % 8 if direction == 0 else h]
 
+    def img_part(kb, ka, part):
+        return imgs.at[pl.ds((kb * 4 + ka) * ROWS + part[0], part[1]), :]
+
+    def send_a():
+        for d in (0, 1):
+            links.start(img_at(0, 0), img_at(0, b_key(d)), ta[d], to_a[1 + d])
+
+    def got_a():
+        for d in (0, 1):
+            links.arrived(img_at(0, b_key(d)), ta[d])
+            links.start(img_part(0, b_key(d), CUT[d]), img_part(0, 3, CUT[d]), ta_far[d], to_a[1 + d])
+
+    def got_a_far():
+        for d in (0, 1):
+            links.arrived(img_part(0, 3, CUT[d]), ta_far[d])
+
     def send_b(ka):
         for d in (0, 1):
             links.start(img_at(0, ka), img_at(b_key(d), ka), tb[d][ka], to_b[d])
@@ -166,8 +196,18 @@
     def got_b(ka):
         for d in (0, 1):
             links.arrived(img_at(b_key(d), ka), tb[d][ka])
-            if ka % 2 == d:
-                links.start(img_at(b_key(d), ka), img_at(3, ka), tb_far[ka], to_b[d])
+
+    def send_b_far(ka):
+        for d in (0, 1):
+            part = FAR_PARTS[ka][d]
+            if part:
+                links.start(img_part(b_key(d), ka, part), img_part(3, ka, part), tb_far[ka][d], to_b[d])
+
+    def got_b_far(ka):
+        for d in (0, 1):
+            part = FAR_PARTS[ka][d]
+            if part:
+                links.arrived(img_part(3, ka, part), tb_far[ka][d])
 
     def send_z(d, h, p):
         first, count = PIECES[p]
@@ -178,15 +218,15 @@
             to_z[d],
         )
 
-    def got_z(h):
-        for p in (0, 2, 1):
-            for d in (0, 1):
-                if h == 4 and p not in FULL[d]:
-                    continue
-                first, count = PIECES[p]
-                links.arrived(txt_at(z_key(d, h), 0, first, count), tz[d][h - 1][p])
-                if h < 3 or (h == 3 and p in FULL[d]):
-                    send_z(d, h + 1, p)
+    def got_z(h, p):
+        for d in (0, 1):
+            if h == 4 and p not in FULL[d]:
+                continue
+            first, count = PIECES[p]
+            links.arrived(txt_at(z_key(d, h), 0, first, count), tz[d][h - 1][p])
+            if h < 3 or (h == 3 and p in FULL[d]):
+                send_z(d, h + 1, p)
+
 
     def send_sib(kz):
         links.start(txt_at(kz, 0), txt_at(kz, 1), t_sib[kz], sibling)
@@ -194,16 +234,10 @@
     def got_sib(kz):
         links.arrived(txt_at(kz, 1), t_sib[kz])
 
+    send_a()
     for p in (0, 2, 1):
         for d in (0, 1):
             send_z(d, 1, p)
-    for ka in (3, 1, 2):
-        off = OFF4[ka]
-        links.start(img_at(0, 0), img_at(0, KEY4[-off % 4]), ta[ka], to_a[ka])
-    send_b(0)
-    send_sib(0)
-    for k in (1, 2, 3):
-        links.start(mates.at[x], mates.at[x], t_mates[k - 1], partners[k - 1])
 
     column = lax.broadcasted_iota(jnp.int32, (8, SIDE), 1)
     ids = column
@@ -215,13 +249,24 @@
             ids = jnp.where(column >= slot * ROWS, column - slot * ROWS + start, ids)
     text_ids[...] = ids.astype(F32)
 
-    got_z(1)
+    for copy in links.open[0:2]:
+        copy.wait_send()
+    links.open = links.open[2:]
+    send_b(0)
+    send_sib(0)
+    for k in (1, 2, 3):
+        links.start(mates.at[x], mates.at[x], t_mates[k - 1], partners[k - 1])
+    got_z(1, 0)
+    got_a()
+    send_b(1)
+    send_b(2)
+    got_z(1, 2)
+    got_z(1, 1)
     send_sib(1)
     send_sib(2)
-    for ka in (1, 2, 3):
-        links.arrived(img_at(0, KEY4[-OFF4[ka] % 4]), ta[ka])
-        send_b(KEY4[-OFF4[ka] % 4])
-    got_b(0)
+    got_a_far()
+    send_b(3)
+    got_z(2, 0)
 
     for k in (1, 2, 3):
         links.arrived(mates.at[(x + 4 - k) % 4], t_mates[k - 1])
@@ -240,9 +285,9 @@
             start = pl.multiple_of((2 * py + core) * ROWS, 16)
             mate_cols[(kb * 4 + ka) * ROWS:(kb * 4 + ka + 1) * ROWS, :] = mate_all[px, pl.ds(start, ROWS), :]
 
-    scale = jnp.exp(jnp.full((1, 1), log_scale_ref[0], F32))
+    scale = jnp.exp(log_scale_ref[...])
     to_log2 = scale * math.log2(math.e)
-    shift = jnp.full((1, 1), bias_ref[0] * math.log2(math.e), F32)
+    shift = bias_ref[...] * math.log2(math.e)
 
     def tile(kb, first, count):
         rows = pl.ds(kb * BUNDLE if isinstance(kb, int) else pl.multiple_of(kb * BUNDLE, BUNDLE), BUNDLE)
@@ -267,6 +312,16 @@
             folded = folded + total[:, k:k + 128]
         loss_acc[...] += folded
 
+    def text_part(first, count, low, high):
+        rows, depth = pl.ds(first, count), pl.ds(low, high - low)
+        part = lax.dot_general(
+            slopes[depth, rows], imgs[depth, :], (((0,), (0,)), ((), ())), preferred_element_type=F32
+        )
+        if low:
+            ptxt[rows, :] += part
+        else:
+            ptxt[rows, :] = part
+
     def tiles(low, high, first, count):
         def step(kb, _):
             tile(kb, first, count)
@@ -274,31 +329,41 @@
 
         lax.fori_loop(low, high, step, 0)
 
+    got_z(2, 2)
+    got_z(2, 1)
+    send_sib(3)
+    send_sib(4)
     got_sib(0)
     got_sib(1)
     tile(0, 0, 256)
-    got_z(2)
-    send_sib(3)
-    send_sib(4)
     got_b(1)
+    send_b_far(1)
     got_b(2)
+    send_b_far(2)
+    got_b(0)
+    send_b_far(0)
+    got_z(3, 0)
+    got_z(3, 2)
+    got_z(3, 1)
+    send_sib(5)
+    send_sib(6)
     got_sib(2)
     got_sib(3)
     got_sib(4)
     tile(0, 256, 512)
-    got_z(3)
-    send_sib(5)
-    send_sib(6)
     got_b(3)
+    send_b_far(3)
     tiles(1, 3, 0, 768)
-    got_z(4)
+    for p in (0, 2, 1):
+        got_z(4, p)
     send_sib(7)
     got_sib(5)
     got_sib(6)
     got_sib(7)
     tiles(0, 3, 768, 512)
-    for ka in range(4):
-        links.arrived(img_at(3, ka), tb_far[ka])
+    text_part(768, 512, 0, 960)
+    for ka in (2, 1, 0, 3):
+        got_b_far(ka)
     tile(3, 0, 1280)
 
     lx, ly, lz, lc = links.tickets(3), links.tickets(3), links.tickets(7), links.tickets(1)
@@ -319,12 +384,6 @@
         rows = pl.ds(kb * BUNDLE, BUNDLE)
         pimg[rows, :] = jnp.dot(slopes[rows, :], txts[...], preferred_element_type=F32)
 
-    def text_part(first, count):
-        rows = pl.ds(first, count)
-        ptxt[rows, :] = lax.dot_general(
-            slopes[:, rows], imgs[...], (((0,), (0,)), ((), ())), preferred_element_type=F32
-        )
-
     whole = pl.ds(0, ROWS)
 
     def send_pair(q, s, q_in, s_in, tickets, device):
@@ -422,18 +481,14 @@
             z_piece(z_q, d, r, p), z_s.at[n], z_piece(z_qi, d, r, p), z_si.at[n], u_z[d][r - 1][p], to_z[d]
         )
 
-    image_part(3)
-    send_far()
     part = jnp.sum(jnp.sum(loss_acc[...], axis=0, keepdims=True), axis=1, keepdims=True)
     loss_x[x] = jnp.broadcast_to(part, (8, 128))
     share(loss_x, x, 4, lx, partners[0:3])
-    text_part(768, 512)
+    text_part(768, 512, 960, 1280)
     for kz in (7, 5, 6):
         swap_text(kz)
-    image_part(1)
-    image_part(2)
-    send_near(0, 1)
-    send_near(1, 3)
+    image_part(3)
+    send_far()
     got_swap(7)
     for p, d in ((0, 0), (2, 1), (1, 0)):
         send_zsum(d, 4, p)
@@ -441,36 +496,40 @@
     got_swap(6)
     for p, d in ((2, 0), (0, 1), (1, 1)):
         send_zsum(d, 3, p)
+    image_part(1)
+    send_near(0, 1)
+    image_part(2)
+    send_near(1, 3)
+    loss_y[y] = gathered(loss_x, x, 4, lx)
+    share(loss_y, y, 4, ly, partners[3:6])
     send_near(0, 3)
     send_near(1, 1)
-    send_near(0, 0)
+    for p, d in ((0, 0), (2, 1), (1, 0)):
+        send_zsum(d, 3, p)
     send_near(1, 2)
-    text_part(256, 512)
+    send_near(0, 2)
+    text_part(256, 512, 0, 1280)
     for kz in (3, 4, 2):
         swap_text(kz)
-    loss_y[y] = gathered(loss_x, x, 4, lx)
-    share(loss_y, y, 4, ly, partners[3:6])
-    send_near(0, 2)
+    send_near(0, 0)
     send_near(1, 0)
-    for p, d in ((0, 0), (2, 1), (1, 0)):
-        send_zsum(d, 3, p)
-    text_part(0, 256)
-    for kz in (1, 0):
-        swap_text(kz)
-    image_part(0)
-    loss_z[z] = gathered(loss_y, y, 4, ly)
-    share(loss_z, z, 8, lz, partners[6:13])
     got_swap(3)
     got_swap(4)
     for p, d in ((2, 0), (0, 1), (1, 1), (0, 0), (2, 1), (1, 0)):
         send_zsum(d, 2, p)
+    image_part(0)
     fold(3)
     fold(1)
+    text_part(0, 256, 0, 1280)
+    for kz in (1, 0):
+        swap_text(kz)
+    loss_z[z] = gathered(loss_y, y, 4, ly)
+    share(loss_z, z, 8, lz, partners[6:13])
+    fold(2)
     got_swap(1)
     got_swap(2)
     for p, d in ((2, 0), (0, 1), (1, 1), (0, 0), (2, 1), (1, 0)):
         send_zsum(d, 1, p)
-    fold(2)
     fold(0)
     loss_c[core] = gathered(loss_z, z, 8, lz)
     share(loss_c, core, 2, lc, [sibling])
@@ -483,11 +542,9 @@
         v = pimg[0:ROWS, lanes]
         for ka in (1, 2, 3):
             v = v + widen(a_qi.at[ka], a_si.at[ka], whole, lanes)
-        pimg[0:ROWS, lanes] = v
+        image_dir_ref[:, lanes] = v * scale
 
     by_lanes(image_sum)
-    unit, inverse = normalize(image_ref[...])
-    grad_image_ref[...] = back_norm(unit, inverse, scale * pimg[0:ROWS, :])
 
     for p, d in ((2, 0), (0, 1), (1, 1), (0, 0), (2, 1), (1, 0)):
         got_zsum(d, 1, p)
@@ -498,29 +555,27 @@
             v = ptxt[here, lanes] + widen(sib_qi.at[0], sib_si.at[0], here, lanes)
             for d in (0, 1):
                 v = v + widen(z_qi.at[d * 4], z_si.at[z_step(d, 1, p)], here, lanes)
-            ptxt[here, lanes] = v
+            text_dir_ref[here, lanes] = v * scale
 
     by_lanes(text_sum)
-    unit, inverse = normalize(text_ref[...])
-    grad_text_ref[...] = back_norm(unit, inverse, scale * ptxt[0:ROWS, :])
     loss_ref[...] = gathered(loss_c, core, 2, lc) * (1.0 / PAIRS)
     links.drain()
 
 
 def on_device(image_emb, text_emb, partner, log_scale, bias):
-    vmem, smem = pl.BlockSpec(memory_space=pltpu.VMEM), pl.BlockSpec(memory_space=pltpu.SMEM)
+    vmem = pl.BlockSpec(memory_space=pltpu.VMEM)
 
     def messages(count):
         return [pltpu.VMEM((count, ROWS, D), I16), pltpu.VMEM((count, 1, D), F32)] * 2
 
-    loss, grad_image, grad_text = pl.pallas_call(
+    loss, image_dir, text_dir = pl.pallas_call(
         kernel,
         out_shape=(
             jax.ShapeDtypeStruct((8, 128), F32),
             jax.ShapeDtypeStruct((ROWS, D), F32),
             jax.ShapeDtypeStruct((ROWS, D), F32),
         ),
-        in_specs=[vmem, vmem, vmem, smem, smem],
+        in_specs=[vmem] * 5,
         out_specs=(vmem, vmem, vmem),
         scratch_shapes=[
             pltpu.VMEM((SIDE, D), BF16),
@@ -549,8 +604,18 @@
         compiler_params=pltpu.CompilerParams(
             collective_id=0, has_side_effects=True, vmem_limit_bytes=60 * 1024 * 1024
         ),
-    )(image_emb, text_emb, partner.reshape(20, 128), log_scale, bias)
-    return (loss[0, 0:1], grad_image, grad_text)
+    )(image_emb, text_emb, partner.reshape(20, 128), log_scale.reshape(1, 1), bias.reshape(1, 1))
+    loss, grad_image, grad_text = pl.pallas_call(
+        finish,
+        out_shape=(
+            jax.ShapeDtypeStruct((1, 1), F32),
+            jax.ShapeDtypeStruct((ROWS, D), F32),
+            jax.ShapeDtypeStruct((ROWS, D), F32),
+        ),
+        in_specs=[vmem] * 5,
+        out_specs=(vmem, vmem, vmem),
+    )(image_emb, text_emb, loss, image_dir, text_dir)
+    return (loss.reshape(1), grad_image, grad_text)
 
 
 def solution(mesh):

time: 76.6 us -> 73.8 us (0.963)
  local copies, waits for them, and re-layouts: 3.73 us -> 0 us
  Pallas kernels: 70.8 us -> 71.7 us
    unnamed x4 -> x0, local copies, waits for them, and re-layouts: 2.54 us -> none
    pallas_call x0 -> x1, Pallas kernels: none -> 2.34 us  [on_device(): pl.pallas_call(finish, out_shape=(jax.ShapeDtypeStruct((1, 1), F32), jax....]
    pallas_call x1, Pallas kernels: 70.8 us -> 69.3 us  [on_device(): pl.pallas_call(kernel, out_shape=(jax.ShapeDtypeStruct((8, 128), F32), ja...]
    slice x1 -> x0, local copies, waits for them, and re-layouts: 1.19 us -> none  [on_device(): return (loss[0, 0:1], grad_image, grad_text)]
where the time goes in v3:
time: 73.8 us; the launch traced here: 73.6 us
  Pallas kernels  71.7 us (97%)
  between operations  1.93 us (3%)
    pallas_call x1, Pallas kernels, on_device(): pl.pallas_call(kernel, out_shape=(jax.ShapeDtypeStruct((8, 128), F32), ja...  69.3 us
    pallas_call x1, Pallas kernels, on_device(): pl.pallas_call(finish, out_shape=(jax.ShapeDtypeStruct((1, 1), F32), jax....  2.34 us

profile of v3, /device:TPU:1, one launch (start us, length us, event | category | flops | bytes accessed | tf_op | source)
XLA Modules:
  0.0 73.6 jit_solution(8984562731609637122)
XLA Ops:
  1.9 69.3 %shard_map.76 = (f32[8,128]{1,0:T(8,128)}, f32[80,1152]{1,0:T(8,128)}, f32[80,1152]{1,0:T(8,128)}) custom-call(bf16[80,1152]{1,0:T(8,128)(2,1)} %image_ref.3, bf16[80,1152]{1,0:T(8,128)(2,1)} %text_ref.3, s32[20,128]{1,0:T(8,128)} %bitcast.6, f32[1,1]{1,0:T(1,128)} %bitcast.4.log_scale_ref, f32[1,1]{1,0:T(1,128)} %bitcast.5.bias_ref), custom_call_target="tpu_custom_call" | custom-call | tf_op jit(solution)/shard_map/pallas_call | solution.py:571
  71.3 2.3 %shard_map.77 = (f32[1,1]{1,0:T(1,128)}, f32[80,1152]{1,0:T(8,128)}, f32[80,1152]{1,0:T(8,128)}) custom-call(bf16[80,1152]{1,0:T(8,128)(2,1)} %image_ref.3, bf16[80,1152]{1,0:T(8,128)(2,1)} %text_ref.3, f32[8,128]{1,0:T(8,128)} %get-tuple-element.9.loss_part_ref, f32[80,1152]{1,0:T(8,128)} %get-tuple-element.10.image_dir_ref, ...), custom_call_target="tpu_custom_call" | custom-call | tf_op jit(solution)/shard_map/pallas_call | solution.py:608

commit v4 on v3

--- a/solution.py
+++ b/solution.py
@@ -17,8 +17,8 @@
 OFF8 = (0, 1, 7, 2, 6, 3, 5, 4)
 KEY4 = {off: k for k, off in enumerate(OFF4)}
 KEY8 = {off: k for k, off in enumerate(OFF8)}
-PIECES = ((0, 32), (32, 16), (48, 32))
-FULL = ((0, 1), (2,))
+PIECES = ((0, 48), (48, 32))
+FULL = ((0,), (1,))
 CUT = ((0, 48), (48, 32))
 FAR_PARTS = (((0, 32), (32, 48)), (None, (0, 80)), ((0, 80), None), CUT)
 COUNT = 224
@@ -81,12 +81,13 @@
     return q[rows, lanes].astype(F32) * s[:, lanes]
 
 
-def narrow(value, q, s, rows):
+def narrow(items):
     def body(lanes):
-        v = value(lanes)
-        top = jnp.maximum(jnp.max(jnp.abs(v), axis=0, keepdims=True), 1e-30)
-        q[rows, lanes] = jnp.round(v * (32767.0 * pltpu.reciprocal(top, approx=True))).astype(I16)
-        s[:, lanes] = top * (1.0 / 32767.0)
+        for value, q, s, rows in items:
+            v = value(lanes)
+            top = jnp.maximum(jnp.max(jnp.abs(v), axis=0, keepdims=True), 1e-30)
+            q[rows, lanes] = jnp.round(v * (32767.0 * pltpu.reciprocal(top, approx=True))).astype(I16)
+            s[:, lanes] = top * (1.0 / 32767.0)
 
     by_lanes(body)
 
@@ -102,8 +103,9 @@
 
 
 def kernel(
-    image_ref, text_ref, table_ref, log_scale_ref, bias_ref,
+    image_hbm, text_hbm, table_hbm, log_scale_hbm, bias_hbm,
     loss_ref, image_dir_ref, text_dir_ref,
+    image_ref, text_ref, table_ref, log_scale_ref, bias_ref, load_sems,
     imgs, txts, slopes, pimg, ptxt,
     mates, mate_rows, mate_all, mate_cols, text_ids, loss_acc,
     far_q, far_s, far_qi, far_si,
@@ -147,8 +149,20 @@
     for device in partners:
         pl.semaphore_signal(barrier, inc=1, device_id=device, device_id_type=MESH)
 
+    loads = [
+        pltpu.make_async_copy(src, dst, load_sems.at[k])
+        for k, (src, dst) in enumerate((
+            (image_hbm, image_ref), (text_hbm, text_ref), (table_hbm, table_ref),
+            (log_scale_hbm, log_scale_ref), (bias_hbm, bias_ref),
+        ))
+    ]
+    for load in loads:
+        load.start()
+    loads[0].wait()
     imgs[0:ROWS, :] = normalize(image_ref[...])[0].astype(BF16)
+    loads[1].wait()
     txts[0:ROWS, :] = normalize(text_ref[...])[0].astype(BF16)
+    loads[2].wait()
     for k in range(5):
         mates[x, k:k + 1, :] = table_ref[pl.ds(z_lo * 5 + k, 1), :]
     loss_acc[...] = jnp.zeros_like(loss_acc)
@@ -163,7 +177,7 @@
     ta, ta_far = links.tickets(2), links.tickets(2)
     tb = [links.tickets(4) for _ in range(2)]
     tb_far = [links.tickets(2) for _ in range(4)]
-    tz = [[links.tickets(3) for _ in range(4)] for _ in range(2)]
+    tz = [[links.tickets(2) for _ in range(4)] for _ in range(2)]
     t_sib = links.tickets(8)
     t_mates = links.tickets(3)
 
@@ -235,7 +249,7 @@
         links.arrived(txt_at(kz, 1), t_sib[kz])
 
     send_a()
-    for p in (0, 2, 1):
+    for p in (0, 1):
         for d in (0, 1):
             send_z(d, 1, p)
 
@@ -260,14 +274,6 @@
     got_a()
     send_b(1)
     send_b(2)
-    got_z(1, 2)
-    got_z(1, 1)
-    send_sib(1)
-    send_sib(2)
-    got_a_far()
-    send_b(3)
-    got_z(2, 0)
-
     for k in (1, 2, 3):
         links.arrived(mates.at[(x + 4 - k) % 4], t_mates[k - 1])
     mate_rows[...] = jnp.zeros_like(mate_rows)
@@ -285,12 +291,21 @@
             start = pl.multiple_of((2 * py + core) * ROWS, 16)
             mate_cols[(kb * 4 + ka) * ROWS:(kb * 4 + ka + 1) * ROWS, :] = mate_all[px, pl.ds(start, ROWS), :]
 
-    scale = jnp.exp(log_scale_ref[...])
+    got_z(1, 1)
+    send_sib(1)
+    send_sib(2)
+    got_a_far()
+    send_b(3)
+    got_z(2, 0)
+
+    loads[3].wait()
+    loads[4].wait()
+    scale = jnp.exp(jnp.full((1, 1), log_scale_ref[0], F32))
     to_log2 = scale * math.log2(math.e)
-    shift = bias_ref[...] * math.log2(math.e)
-
-    def tile(kb, first, count):
-        rows = pl.ds(kb * BUNDLE if isinstance(kb, int) else pl.multiple_of(kb * BUNDLE, BUNDLE), BUNDLE)
+    shift = jnp.full((1, 1), bias_ref[0] * math.log2(math.e), F32)
+
+    def tile(kb, top, height, first, count):
+        rows = pl.ds(kb * BUNDLE + top if isinstance(kb, int) else pl.multiple_of(kb * BUNDLE + top, 16), height)
         cols = pl.ds(first, count)
         cosine = lax.dot_general(
             imgs[rows, :], txts[cols, :], (((1,), (1,)), ((), ())), preferred_element_type=F32
@@ -302,17 +317,21 @@
         mate = mate_cols[rows, :]
         positive = jnp.concatenate([mate] * (count // 128), axis=1) == text_ids[0:1, cols]
         slopes[rows, cols] = jnp.where(positive, -r, e * r).astype(BF16)
-        lost = (e - (u - 1.0)) * r
         paired = jnp.where(positive, logits, 0.0)
-        product = u[0:80] * u[80:160] * u[160:240] * u[240:320]
-        total = jnp.log(product).reshape(10, 8, count).sum(0)
-        total += lost.reshape(40, 8, count).sum(0) - paired.reshape(40, 8, count).sum(0) * math.log(2.0)
+        grown = [e[k:k + ROWS] for k in range(0, height, ROWS)]
+        while len(grown) > 1:
+            first_e, second_e, *others = grown
+            grown = [*others, first_e + second_e + first_e * second_e]
+        over = 1.0 + grown[0]
+        lost = jnp.log(over) + (grown[0] - (over - 1.0)) * pltpu.reciprocal(over, approx=True)
+        total = lost.reshape(10, 8, count).sum(0)
+        total -= paired.reshape(height // 8, 8, count).sum(0) * math.log(2.0)
         folded = total[:, 0:128]
         for k in range(128, count, 128):
             folded = folded + total[:, k:k + 128]
         loss_acc[...] += folded
 
-    def text_part(first, count, low, high):
+    def text_part(first, count, low=0, high=SIDE):
         rows, depth = pl.ds(first, count), pl.ds(low, high - low)
         part = lax.dot_general(
             slopes[depth, rows], imgs[depth, :], (((0,), (0,)), ((), ())), preferred_element_type=F32
@@ -322,49 +341,41 @@
         else:
             ptxt[rows, :] = part
 
-    def tiles(low, high, first, count):
+    def tiles(low, high, top, height, first, count):
         def step(kb, _):
-            tile(kb, first, count)
+            tile(kb, top, height, first, count)
             return 0
 
         lax.fori_loop(low, high, step, 0)
 
-    got_z(2, 2)
     got_z(2, 1)
     send_sib(3)
     send_sib(4)
-    got_sib(0)
-    got_sib(1)
-    tile(0, 0, 256)
     got_b(1)
     send_b_far(1)
     got_b(2)
     send_b_far(2)
     got_b(0)
     send_b_far(0)
+    for kz in (0, 1, 2, 3, 4):
+        got_sib(kz)
+    tile(0, 0, BUNDLE, 0, 768)
     got_z(3, 0)
-    got_z(3, 2)
     got_z(3, 1)
     send_sib(5)
     send_sib(6)
-    got_sib(2)
-    got_sib(3)
-    got_sib(4)
-    tile(0, 256, 512)
     got_b(3)
     send_b_far(3)
-    tiles(1, 3, 0, 768)
-    for p in (0, 2, 1):
+    tiles(1, 3, 0, BUNDLE, 0, 768)
+    text_part(0, 384, 0, 960)
+    for p in (0, 1):
         got_z(4, p)
     send_sib(7)
+    text_part(384, 384, 0, 960)
     got_sib(5)
     got_sib(6)
     got_sib(7)
-    tiles(0, 3, 768, 512)
-    text_part(768, 512, 0, 960)
-    for ka in (2, 1, 0, 3):
-        got_b_far(ka)
-    tile(3, 0, 1280)
+    tiles(0, 3, 0, BUNDLE, 768, 512)
 
     lx, ly, lz, lc = links.tickets(3), links.tickets(3), links.tickets(7), links.tickets(1)
 
@@ -402,32 +413,46 @@
     u_near = [{ka: links.tickets(2) for ka in range(4)} for _ in range(2)]
     u_a = {ka: links.tickets(2) for ka in (1, 2, 3)}
     u_sib = [links.tickets(2) for _ in range(8)]
-    u_z = [[[links.tickets(2) for _ in range(3)] for _ in range(4)] for _ in range(2)]
-
-    def send_far():
-        for n in (0, 1):
-            for d in (0, 1):
-                ka = FAR[d][n]
-                narrow(lambda lanes: pimg[img_rows(3, ka), lanes], far_q.at[ka], far_s.at[ka], whole)
-                send_pair(far_q.at[ka], far_s.at[ka], far_qi.at[ka], far_si.at[ka], u_far[ka], to_b[d])
-
-    def send_near(d, ka):
-        kb = KEY4[1 if d == 0 else 3]
-        added = ka in FAR[d]
-        if added:
-            got_pair(far_qi.at[ka], far_si.at[ka], u_far[ka])
-
-        def value(lanes):
-            v = pimg[img_rows(kb, ka), lanes]
-            return v + widen(far_qi.at[ka], far_si.at[ka], whole, lanes) if added else v
-
-        n = d * 4 + ka
-        narrow(value, near_q.at[n], near_s.at[n], whole)
-        send_pair(near_q.at[n], near_s.at[n], near_qi.at[n], near_si.at[n], u_near[d][ka], to_b[d])
+    u_z = [[[links.tickets(2) for _ in range(2)] for _ in range(4)] for _ in range(2)]
+
+    def send_far(n):
+        items = []
+        for d in (0, 1):
+            rows = img_rows(3, FAR[d][n])
+            items.append((lambda lanes, rows=rows: pimg[rows, lanes], far_q.at[FAR[d][n]], far_s.at[FAR[d][n]], whole))
+        narrow(items)
+        for d in (0, 1):
+            ka = FAR[d][n]
+            send_pair(far_q.at[ka], far_s.at[ka], far_qi.at[ka], far_si.at[ka], u_far[ka], to_b[d])
+
+    sent_near = []
+
+    def send_near(pairs):
+        items = []
+        for d, ka in pairs:
+            rows = img_rows(KEY4[1 if d == 0 else 3], ka)
+            if ka in FAR[d]:
+                got_pair(far_qi.at[ka], far_si.at[ka], u_far[ka])
+
+            def value(lanes, d=d, ka=ka, rows=rows):
+                v = pimg[rows, lanes]
+                return v + widen(far_qi.at[ka], far_si.at[ka], whole, lanes) if ka in FAR[d] else v
+
+            items.append((value, near_q.at[d * 4 + ka], near_s.at[d * 4 + ka], whole))
+        narrow(items)
+        for d in (0, 1):
+            kas = [ka for e, ka in pairs if e == d]
+            if kas:
+                n = pl.ds(d * 4 + min(kas), len(kas))
+                send_pair(near_q.at[n], near_s.at[n], near_qi.at[n], near_si.at[n], u_near[d][min(kas)], to_b[d])
+                sent_near.append((d, tuple(kas)))
 
     def fold(ka):
-        for d in (0, 1):
-            got_pair(near_qi.at[d * 4 + ka], near_si.at[d * 4 + ka], u_near[d][ka])
+        for d, kas in list(sent_near):
+            if ka in kas:
+                n = pl.ds(d * 4 + min(kas), len(kas))
+                got_pair(near_qi.at[n], near_si.at[n], u_near[d][min(kas)])
+                sent_near.remove((d, kas))
 
         def value(lanes):
             v = pimg[img_rows(0, ka), lanes]
@@ -436,7 +461,7 @@
             )
 
         if ka:
-            narrow(value, a_q.at[ka], a_s.at[ka], whole)
+            narrow([(value, a_q.at[ka], a_s.at[ka], whole)])
             send_pair(a_q.at[ka], a_s.at[ka], a_qi.at[ka], a_si.at[ka], u_a[ka], to_a[ka])
         else:
             def body(lanes):
@@ -444,10 +469,14 @@
 
             by_lanes(body)
 
-    def swap_text(kz):
-        rows = pl.ds((kz * 2 + 1) * ROWS, ROWS)
-        narrow(lambda lanes: ptxt[rows, lanes], sib_q.at[kz], sib_s.at[kz], whole)
-        send_pair(sib_q.at[kz], sib_s.at[kz], sib_qi.at[kz], sib_si.at[kz], u_sib[kz], sibling)
+    def swap_text(keys):
+        items = []
+        for kz in keys:
+            rows = pl.ds((kz * 2 + 1) * ROWS, ROWS)
+            items.append((lambda lanes, rows=rows: ptxt[rows, lanes], sib_q.at[kz], sib_s.at[kz], whole))
+        narrow(items)
+        for kz in keys:
+            send_pair(sib_q.at[kz], sib_s.at[kz], sib_qi.at[kz], sib_si.at[kz], u_sib[kz], sibling)
 
     def got_swap(kz):
         got_pair(sib_qi.at[kz], sib_si.at[kz], u_sib[kz])
@@ -456,80 +485,78 @@
         return buffer.at[d * 4 + r - 1, pl.ds(*PIECES[p]), :]
 
     def z_step(d, r, p):
-        return (d * 4 + r - 1) * 3 + p
+        return (d * 4 + r - 1) * 2 + p
 
     def got_zsum(d, r, p):
         got_pair(z_piece(z_qi, d, r, p), z_si.at[z_step(d, r, p)], u_z[d][r - 1][p])
 
-    def send_zsum(d, r, p):
-        first, count = PIECES[p]
-        kz = KEY8[r % 8 if d == 0 else -r % 8]
-        added = r < 3 or (r == 3 and p in FULL[d])
-        if added:
-            got_zsum(d, r + 1, p)
-        here = pl.ds(first, count)
-
-        def value(lanes):
-            v = ptxt[pl.ds(kz * 2 * ROWS + first, count), lanes] + widen(sib_qi.at[kz], sib_si.at[kz], here, lanes)
+    LONG, SHORT = ((0, 0), (1, 1)), ((1, 0), (0, 1))
+
+    def send_zsum(r, chains):
+        items = []
+        for p, d in chains:
+            first, count = PIECES[p]
+            kz = KEY8[r % 8 if d == 0 else -r % 8]
+            added = r < 3 or (r == 3 and p in FULL[d])
             if added:
-                v = v + widen(z_qi.at[d * 4 + r], z_si.at[z_step(d, r + 1, p)], here, lanes)
-            return v
-
-        n = z_step(d, r, p)
-        narrow(value, z_q.at[d * 4 + r - 1], z_s.at[n], here)
-        send_pair(
-            z_piece(z_q, d, r, p), z_s.at[n], z_piece(z_qi, d, r, p), z_si.at[n], u_z[d][r - 1][p], to_z[d]
-        )
-
+                got_zsum(d, r + 1, p)
+            here = pl.ds(first, count)
+
+            def value(lanes, d=d, p=p, first=first, count=count, kz=kz, added=added, here=here):
+                v = ptxt[pl.ds(kz * 2 * ROWS + first, count), lanes] + widen(sib_qi.at[kz], sib_si.at[kz], here, lanes)
+                if added:
+                    v = v + widen(z_qi.at[d * 4 + r], z_si.at[z_step(d, r + 1, p)], here, lanes)
+                return v
+
+            items.append((value, z_q.at[d * 4 + r - 1], z_s.at[z_step(d, r, p)], here))
+        narrow(items)
+        for p, d in chains:
+            n = z_step(d, r, p)
+            send_pair(
+                z_piece(z_q, d, r, p), z_s.at[n], z_piece(z_qi, d, r, p), z_si.at[n], u_z[d][r - 1][p], to_z[d]
+            )
+
+    for ka in (2, 1, 0, 3):
+        got_b_far(ka)
+    tile(3, 0, BUNDLE, 0, SIDE)
+    text_part(768, 512)
+    swap_text((7, 5, 6))
+    image_part(3)
+    send_far(0)
+    send_far(1)
+    got_swap(7)
+    send_zsum(4, LONG)
+    got_swap(5)
+    got_swap(6)
+    send_zsum(3, SHORT)
     part = jnp.sum(jnp.sum(loss_acc[...], axis=0, keepdims=True), axis=1, keepdims=True)
     loss_x[x] = jnp.broadcast_to(part, (8, 128))
     share(loss_x, x, 4, lx, partners[0:3])
-    text_part(768, 512, 960, 1280)
-    for kz in (7, 5, 6):
-        swap_text(kz)
-    image_part(3)
-    send_far()
-    got_swap(7)
-    for p, d in ((0, 0), (2, 1), (1, 0)):
-        send_zsum(d, 4, p)
-    got_swap(5)
-    got_swap(6)
-    for p, d in ((2, 0), (0, 1), (1, 1)):
-        send_zsum(d, 3, p)
     image_part(1)
-    send_near(0, 1)
+    send_near(((0, 1), (0, 0)))
     image_part(2)
-    send_near(1, 3)
+    send_near(((1, 3), (1, 2)))
+    text_part(0, 768, 960, SIDE)
+    swap_text((3, 4, 2, 1, 0))
+    image_part(0)
+    send_zsum(3, LONG)
+    send_near(((0, 3), (1, 1)))
     loss_y[y] = gathered(loss_x, x, 4, lx)
     share(loss_y, y, 4, ly, partners[3:6])
-    send_near(0, 3)
-    send_near(1, 1)
-    for p, d in ((0, 0), (2, 1), (1, 0)):
-        send_zsum(d, 3, p)
-    send_near(1, 2)
-    send_near(0, 2)
-    text_part(256, 512, 0, 1280)
-    for kz in (3, 4, 2):
-        swap_text(kz)
-    send_near(0, 0)
-    send_near(1, 0)
     got_swap(3)
     got_swap(4)
-    for p, d in ((2, 0), (0, 1), (1, 1), (0, 0), (2, 1), (1, 0)):
-        send_zsum(d, 2, p)
-    image_part(0)
+    send_zsum(2, SHORT)
+    send_near(((0, 2), (1, 0)))
     fold(3)
-    fold(1)
-    text_part(0, 256, 0, 1280)
-    for kz in (1, 0):
-        swap_text(kz)
+    send_zsum(2, LONG)
     loss_z[z] = gathered(loss_y, y, 4, ly)
     share(loss_z, z, 8, lz, partners[6:13])
-    fold(2)
     got_swap(1)
     got_swap(2)
-    for p, d in ((2, 0), (0, 1), (1, 1), (0, 0), (2, 1), (1, 0)):
-        send_zsum(d, 1, p)
+    send_zsum(1, SHORT)
+    fold(1)
+    fold(2)
+    send_zsum(1, LONG)
     fold(0)
     loss_c[core] = gathered(loss_z, z, 8, lz)
     share(loss_c, core, 2, lc, [sibling])
@@ -546,7 +573,7 @@
 
     by_lanes(image_sum)
 
-    for p, d in ((2, 0), (0, 1), (1, 1), (0, 0), (2, 1), (1, 0)):
+    for p, d in (*SHORT, *LONG):
         got_zsum(d, 1, p)
 
     def text_sum(lanes):
@@ -575,9 +602,15 @@
             jax.ShapeDtypeStruct((ROWS, D), F32),
             jax.ShapeDtypeStruct((ROWS, D), F32),
         ),
-        in_specs=[vmem] * 5,
+        in_specs=[pl.BlockSpec(memory_space=pl.ANY)] * 5,
         out_specs=(vmem, vmem, vmem),
         scratch_shapes=[
+            pltpu.VMEM((ROWS, D), BF16),
+            pltpu.VMEM((ROWS, D), BF16),
+            pltpu.VMEM((20, 128), jnp.int32),
+            pltpu.SMEM((1,), F32),
+            pltpu.SMEM((1,), F32),
+            pltpu.SemaphoreType.DMA((5,)),
             pltpu.VMEM((SIDE, D), BF16),
             pltpu.VMEM((SIDE, D), BF16),
             pltpu.VMEM((SIDE, SIDE), BF16),
@@ -593,7 +626,7 @@
             *messages(8),
             *messages(4),
             *messages(8),
-            *[pltpu.VMEM((8, ROWS, D), I16), pltpu.VMEM((24, 1, D), F32)] * 2,
+            *[pltpu.VMEM((8, ROWS, D), I16), pltpu.VMEM((16, 1, D), F32)] * 2,
             pltpu.VMEM((4, 8, 128), F32),
             pltpu.VMEM((4, 8, 128), F32),
             pltpu.VMEM((8, 8, 128), F32),
@@ -604,7 +637,7 @@
         compiler_params=pltpu.CompilerParams(
             collective_id=0, has_side_effects=True, vmem_limit_bytes=60 * 1024 * 1024
         ),
-    )(image_emb, text_emb, partner.reshape(20, 128), log_scale.reshape(1, 1), bias.reshape(1, 1))
+    )(image_emb, text_emb, partner.reshape(20, 128), log_scale, bias)
     loss, grad_image, grad_text = pl.pallas_call(
         finish,
         out_shape=(

time: 73.8 us -> 72 us (0.976)
  Pallas kernels: 71.7 us -> 69.9 us
    pallas_call x1, Pallas kernels: 69.3 us -> 67.5 us  [on_device(): pl.pallas_call(kernel, out_shape=(jax.ShapeDtypeStruct((8, 128), F32), ja...]
where the time goes in v4:
time: 72 us; the launch traced here: 71.8 us
  Pallas kernels  69.9 us (97%)
  between operations  1.93 us (3%)
    pallas_call x1, Pallas kernels, on_device(): pl.pallas_call(kernel, out_shape=(jax.ShapeDtypeStruct((8, 128), F32), ja...  67.5 us
    pallas_call x1, Pallas kernels, on_device(): pl.pallas_call(finish, out_shape=(jax.ShapeDtypeStruct((1, 1), F32), jax....  2.34 us

profile of v4, /device:TPU:1, one launch (start us, length us, event | category | flops | bytes accessed | tf_op | source)
XLA Modules:
  0.0 71.8 jit_solution(2977918412428615891)
XLA Ops:
  1.9 67.5 %shard_map.76 = (f32[8,128]{1,0:T(8,128)}, f32[80,1152]{1,0:T(8,128)}, f32[80,1152]{1,0:T(8,128)}) custom-call(bf16[80,1152]{1,0:T(8,128)(2,1)} %image_ref.1, bf16[80,1152]{1,0:T(8,128)(2,1)} %text_ref.1, s32[20,128]{1,0:T(8,128)} %bitcast.2, f32[1]{0:T(128)S(6)} %copy.8.log_scale_hbm, f32[1]{0:T(128)S(6)} %copy.9.bias_hbm), custom_call_target="tpu_custom_call" | custom-call | tf_op jit(solution)/shard_map/pallas_call | solution.py:598
  69.5 2.3 %shard_map.77 = (f32[1,1]{1,0:T(1,128)}, f32[80,1152]{1,0:T(8,128)}, f32[80,1152]{1,0:T(8,128)}) custom-call(bf16[80,1152]{1,0:T(8,128)(2,1)} %image_ref.1, bf16[80,1152]{1,0:T(8,128)(2,1)} %text_ref.1, f32[8,128]{1,0:T(8,128)} %get-tuple-element.9.loss_part_ref, f32[80,1152]{1,0:T(8,128)} %get-tuple-element.10.image_dir_ref, ...), custom_call_target="tpu_custom_call" | custom-call | tf_op jit(solution)/shard_map/pallas_call | solution.py:641

commit v5 on v4

--- a/solution.py
+++ b/solution.py
@@ -19,6 +19,8 @@
 KEY8 = {off: k for k, off in enumerate(OFF8)}
 PIECES = ((0, 48), (48, 32))
 FULL = ((0,), (1,))
+SUM_PIECES = ((0, 32), (32, 16), (48, 32))
+SUM_FULL = ((0, 1), (2,))
 CUT = ((0, 48), (48, 32))
 FAR_PARTS = (((0, 32), (32, 48)), (None, (0, 80)), ((0, 80), None), CUT)
 COUNT = 224
@@ -413,7 +415,7 @@
     u_near = [{ka: links.tickets(2) for ka in range(4)} for _ in range(2)]
     u_a = {ka: links.tickets(2) for ka in (1, 2, 3)}
     u_sib = [links.tickets(2) for _ in range(8)]
-    u_z = [[[links.tickets(2) for _ in range(2)] for _ in range(4)] for _ in range(2)]
+    u_z = [[[links.tickets(2) for _ in range(3)] for _ in range(4)] for _ in range(2)]
 
     def send_far(n):
         items = []
@@ -482,22 +484,22 @@
         got_pair(sib_qi.at[kz], sib_si.at[kz], u_sib[kz])
 
     def z_piece(buffer, d, r, p):
-        return buffer.at[d * 4 + r - 1, pl.ds(*PIECES[p]), :]
+        return buffer.at[d * 4 + r - 1, pl.ds(*SUM_PIECES[p]), :]
 
     def z_step(d, r, p):
-        return (d * 4 + r - 1) * 2 + p
+        return (d * 4 + r - 1) * 3 + p
 
     def got_zsum(d, r, p):
         got_pair(z_piece(z_qi, d, r, p), z_si.at[z_step(d, r, p)], u_z[d][r - 1][p])
 
-    LONG, SHORT = ((0, 0), (1, 1)), ((1, 0), (0, 1))
+    LONG, MIDDLE, SHORT = ((0, 0), (2, 1)), ((1, 0),), ((2, 0), (0, 1), (1, 1))
 
     def send_zsum(r, chains):
         items = []
         for p, d in chains:
-            first, count = PIECES[p]
+            first, count = SUM_PIECES[p]
             kz = KEY8[r % 8 if d == 0 else -r % 8]
-            added = r < 3 or (r == 3 and p in FULL[d])
+            added = r < 3 or (r == 3 and p in SUM_FULL[d])
             if added:
                 got_zsum(d, r + 1, p)
             here = pl.ds(first, count)
@@ -526,6 +528,7 @@
     send_far(1)
     got_swap(7)
     send_zsum(4, LONG)
+    send_zsum(4, MIDDLE)
     got_swap(5)
     got_swap(6)
     send_zsum(3, SHORT)
@@ -538,9 +541,10 @@
     send_near(((1, 3), (1, 2)))
     text_part(0, 768, 960, SIDE)
     swap_text((3, 4, 2, 1, 0))
+    send_zsum(3, LONG)
+    send_zsum(3, MIDDLE)
+    send_near(((0, 3), (1, 1)))
     image_part(0)
-    send_zsum(3, LONG)
-    send_near(((0, 3), (1, 1)))
     loss_y[y] = gathered(loss_x, x, 4, lx)
     share(loss_y, y, 4, ly, partners[3:6])
     got_swap(3)
@@ -549,6 +553,7 @@
     send_near(((0, 2), (1, 0)))
     fold(3)
     send_zsum(2, LONG)
+    send_zsum(2, MIDDLE)
     loss_z[z] = gathered(loss_y, y, 4, ly)
     share(loss_z, z, 8, lz, partners[6:13])
     got_swap(1)
@@ -557,6 +562,7 @@
     fold(1)
     fold(2)
     send_zsum(1, LONG)
+    send_zsum(1, MIDDLE)
     fold(0)
     loss_c[core] = gathered(loss_z, z, 8, lz)
     share(loss_c, core, 2, lc, [sibling])
@@ -573,11 +579,11 @@
 
     by_lanes(image_sum)
 
-    for p, d in (*SHORT, *LONG):
+    for p, d in (*SHORT, *LONG, *MIDDLE):
         got_zsum(d, 1, p)
 
     def text_sum(lanes):
-        for p, (first, count) in enumerate(PIECES):
+        for p, (first, count) in enumerate(SUM_PIECES):
             here = pl.ds(first, count)
             v = ptxt[here, lanes] + widen(sib_qi.at[0], sib_si.at[0], here, lanes)
             for d in (0, 1):
@@ -626,7 +632,7 @@
             *messages(8),
             *messages(4),
             *messages(8),
-            *[pltpu.VMEM((8, ROWS, D), I16), pltpu.VMEM((16, 1, D), F32)] * 2,
+            *[pltpu.VMEM((8, ROWS, D), I16), pltpu.VMEM((24, 1, D), F32)] * 2,
             pltpu.VMEM((4, 8, 128), F32),
             pltpu.VMEM((4, 8, 128), F32),
             pltpu.VMEM((8, 8, 128), F32),

time: 72 us -> 72 us (level)
  no operation moved by 1% of the time
where the time goes in v5:
time: 72 us; the launch traced here: 71.9 us
  Pallas kernels  69.9 us (97%)
  between operations  1.93 us (3%)
    pallas_call x1, Pallas kernels, on_device(): pl.pallas_call(kernel, out_shape=(jax.ShapeDtypeStruct((8, 128), F32), ja...  67.6 us
    pallas_call x1, Pallas kernels, on_device(): pl.pallas_call(finish, out_shape=(jax.ShapeDtypeStruct((1, 1), F32), jax....  2.34 us

profile of v5, /device:TPU:1, one launch (start us, length us, event | category | flops | bytes accessed | tf_op | source)
XLA Modules:
  0.0 71.9 jit_solution(8067434842641622300)
XLA Ops:
  1.9 67.6 %shard_map.76 = (f32[8,128]{1,0:T(8,128)}, f32[80,1152]{1,0:T(8,128)}, f32[80,1152]{1,0:T(8,128)}) custom-call(bf16[80,1152]{1,0:T(8,128)(2,1)} %image_ref.1, bf16[80,1152]{1,0:T(8,128)(2,1)} %text_ref.1, s32[20,128]{1,0:T(8,128)} %bitcast.2, f32[1]{0:T(128)S(6)} %copy.8.log_scale_hbm, f32[1]{0:T(128)S(6)} %copy.9.bias_hbm), custom_call_target="tpu_custom_call" | custom-call | tf_op jit(solution)/shard_map/pallas_call | solution.py:604
  69.5 2.3 %shard_map.77 = (f32[1,1]{1,0:T(1,128)}, f32[80,1152]{1,0:T(8,128)}, f32[80,1152]{1,0:T(8,128)}) custom-call(bf16[80,1152]{1,0:T(8,128)(2,1)} %image_ref.1, bf16[80,1152]{1,0:T(8,128)(2,1)} %text_ref.1, f32[8,128]{1,0:T(8,128)} %get-tuple-element.9.loss_part_ref, f32[80,1152]{1,0:T(8,128)} %get-tuple-element.10.image_dir_ref, ...), custom_call_target="tpu_custom_call" | custom-call | tf_op jit(solution)/shard_map/pallas_call | solution.py:647
